TPU v7x, 32 devices: a whole 2x2x4 slice. The times are simulated.
32 devices in a mesh: wide: 8 (over z, core), narrow: 4 (over y, x).
Axes of the slice: x: 2, y: 2, z: 4, core: 2. Of those that a mesh axis runs over, the one named last changes fastest.
Arguments:
- tokens: bfloat16 [2048, 1024], P('wide', 'narrow'), may hold values from -6 to 6
- gate_weight: bfloat16 [1024, 14784], P('wide', 'narrow'), may hold values from -0.1875 to 0.1875
- up_weight: bfloat16 [1024, 14784], P('wide', 'narrow'), may hold values from -0.1875 to 0.1875
Outputs:
- hidden: bfloat16 [2048, 14784], P('wide', 'narrow')
All inputs are finite; a program needn't handle non-finite values.
Results may differ from a plain program's by a relative error of at most 0.001.
Values may be sent and summed in bfloat16 or wider, within the bound.
No kernel may reach another device: no remote copies, remote signals or barrier semaphores. Data moves between devices by JAX's collectives and lax.ppermute only.
A program may use at most 64 MiB of HBM per device.

v0:
```python
import jax
import jax.numpy as jnp
from jax import lax
from jax.sharding import PartitionSpec as P


def gated(gate, up):
    return (jax.nn.silu(gate) * up).astype(jnp.bfloat16)


def local(tokens, gate_weight, up_weight):
    gathered = lax.all_gather(tokens, "narrow", axis=1, tiled=True)
    row_count = gathered.shape[0]
    width = gathered.shape[1]
    columns_dev = gate_weight.shape[1]
    gate_full = lax.all_gather(gate_weight, "wide", axis=0, tiled=True)
    up_full = lax.all_gather(up_weight, "wide", axis=0, tiled=True)
    block_rows = min(row_count, 256)
    blocks = gathered.reshape(row_count // block_rows, block_rows, width)

    def project_block(rows):
        gate = jnp.dot(rows, gate_full, preferred_element_type=jnp.float32)
        up = jnp.dot(rows, up_full, preferred_element_type=jnp.float32)
        return gated(gate, up)

    return lax.map(project_block, blocks).reshape(row_count, columns_dev)


def solution(mesh):
    in_specs = (P("wide", "narrow"), P("wide", "narrow"), P("wide", "narrow"))
    out_specs = P("wide", "narrow")
    return jax.shard_map(local, mesh=mesh, in_specs=in_specs, out_specs=out_specs, check_vma=False)
```

profile of v0, /device:TPU:0, one launch (start us, length us, event | category | flops | bytes accessed | tf_op | source)
XLA Modules:
  0.0 177.7 jit_solution(3895369340478966120)
XLA Ops:
  6.5 0.0 all-gather.3.cloned.1.call-start
  6.5 0.7 all-gather.3.cloned.1.call-update
  7.3 0.0 all-gather.5.cloned.1.call-start
  7.3 0.7 all-gather.5.cloned.1.call-update
  8.0 15.9 %all_gather.9 = bf16[256,1024]{1,0:T(8,128)(2,1)S(1)} all-gather(bf16[256,256]{1,0:T(8,128)(2,1)} %param.3), channel_id=1, replica_groups=mesh['wide'=8,'narrow'=4] {'narrow'}, dimensions={1}, use_global_device_ids=true | all-gather | bytes 655360 | tf_op jit(solution)/shard_map/all_gather | solution.py:12
  23.9 63.5 %all-gather.3.cloned.1.call-done = bf16[1024,3696]{0,1:T(8,128)(2,1)} async-done(((bf16[128,3696]{0,1:T(8,128)(2,1)}), bf16[1024,3696]{0,1:T(8,128)(2,1)}) %all-gather.3.cloned.1.call-update) | async-done | bytes 7569424 | tf_op jit(solution)/shard_map/all_gather | solution.py:16
  87.4 7.2 %fusion.1 = f32[256,3696]{0,1:T(8,128)} fusion(bf16[256,1024]{1,0:T(8,128)(2,1)S(1)} %all_gather.9, bf16[1024,3696]{0,1:T(8,128)(2,1)} %all-gather.3.cloned.1.call-done), kind=kOutput, calls=%fused_computation.2 | convolution fusion | flops 1937768448 | bytes 11878400 | tf_op jit(solution)/shard_map/while/body/eval_jaxpr/dot_general | solution.py:22
  94.6 68.4 %all-gather.5.cloned.1.call-done = bf16[1024,3696]{0,1:T(8,128)(2,1)} async-done(((bf16[128,3696]{0,1:T(8,128)(2,1)}), bf16[1024,3696]{0,1:T(8,128)(2,1)}) %all-gather.5.cloned.1.call-update) | async-done | bytes 7569424 | tf_op jit(solution)/shard_map/all_gather | solution.py:17
  162.9 7.9 %fusion = bf16[256,3696]{0,1:T(8,128)(2,1)} fusion(bf16[256,1024]{1,0:T(8,128)(2,1)S(1)} %all_gather.9, bf16[1024,3696]{0,1:T(8,128)(2,1)} %all-gather.5.cloned.1.call-done, f32[256,3696]{0,1:T(8,128)} %fusion.1), kind=kOutput, calls=%fused_computation.1 | convolution fusion | flops 1943445504 | bytes 13770752 | tf_op jit(solution)/shard_map/while/body/eval_jaxpr/dot_general | solution.py:23
Async XLA Ops:
  6.5 80.9 %all-gather.3.cloned.1.call-start = ((), (), s32[]{:S(2)}) async-start(), calls=%async_computation | async-start | bytes 8515584 | tf_op jit(solution)/shard_map/all_gather | solution.py:16
  7.3 155.7 %all-gather.5.cloned.1.call-start = ((), (), s32[]{:S(2)}) async-start(), calls=%async_computation.1 | async-start | bytes 8515584 | tf_op jit(solution)/shard_map/all_gather | solution.py:17
Sparse Core Ops, SparseCore 0:
  8.9 78.4 all-gather.2
  89.0 73.9 all-gather.4
where the time goes:
time: 178 us
  waiting for transfers between devices  133 us (75%)
  blocking collectives  15.9 us (9%)
  matrix products  15.1 us (8%)
  between operations  13.4 us (8%)
    all_gather x1, waiting for transfers between devices, local(): up_full = lax.all_gather(up_weight, 'wide', axis=0, tiled=True)  68.4 us
    all_gather x1, waiting for transfers between devices, local(): gate_full = lax.all_gather(gate_weight, 'wide', axis=0, tiled=True)  63.5 us
    all_gather x1, blocking collectives, local(): gathered = lax.all_gather(tokens, 'narrow', axis=1, tiled=True)  15.9 us
    dot_general x1, matrix products, project_block(): up = jnp.dot(rows, up_full, preferred_element_type=jnp.float32)  7.95 us
    dot_general x1, matrix products, project_block(): gate = jnp.dot(rows, gate_full, preferred_element_type=jnp.float32)  7.18 us
  transfers between devices with their start and end apart: 2, of which 2 were waited for; matrix products, arithmetic and copies ran while one was open for 4% of the time, Pallas kernels for 0%

commit v1 on v0

v1 whole, which is shorter than its diff:
```python
import functools

import jax
import jax.numpy as jnp
from jax import lax
from jax.experimental import pallas as pl
from jax.experimental.pallas import tpu as pltpu
from jax.sharding import PartitionSpec as P

CORES = 2
LINE = 4
TILE = 16
SHARES = (46, 46)
TURN = (0, 3, 1, 2)
VMEM = 24 * 1024 * 1024
SMALL = 1024 * 1024
LARGE = 56 * 1024 * 1024


def gated(gate, up):
    return (jax.nn.silu(gate) * up).astype(jnp.bfloat16)


def gathered_everywhere(tokens, gate_weight, up_weight):
    rows = lax.all_gather(tokens, "narrow", axis=1, tiled=True)
    gate_full = lax.all_gather(gate_weight, "wide", axis=0, tiled=True)
    up_full = lax.all_gather(up_weight, "wide", axis=0, tiled=True)
    gate = jnp.dot(rows, gate_full, preferred_element_type=jnp.float32)
    up = jnp.dot(rows, up_full, preferred_element_type=jnp.float32)
    return gated(gate, up)


def line_position():
    index = lax.axis_index("wide")
    return index // CORES, index % CORES


def at_end():
    chip, _ = line_position()
    return (chip == 0) | (chip == LINE - 1)


def half_start(core, columns):
    return pl.multiple_of(core * (columns - half_of(columns)), TILE)


def half_of(columns):
    return -(-columns // (CORES * TILE)) * TILE


def copy_all(copies):
    for copy in copies:
        copy.start()
    for copy in copies:
        copy.wait()


def cut_kernel(gate_ref, up_ref, out_ref, sems):
    _, core = line_position()
    columns = gate_ref.shape[0]
    half = half_of(columns)
    theirs = pl.ds(half_start(1 - core, columns), half)
    copy_all(
        [
            pltpu.make_async_copy(w.at[theirs], out_ref.at[pl.ds(k * half, half)], sems.at[k])
            for k, w in enumerate((gate_ref, up_ref))
        ]
    )


def cut(gate_t, up_t):
    columns, depth = gate_t.shape
    in_hbm = pl.BlockSpec(memory_space=pltpu.HBM)
    return pl.pallas_call(
        cut_kernel,
        in_specs=[in_hbm, in_hbm],
        out_specs=pl.BlockSpec(memory_space=pltpu.VMEM),
        out_shape=jax.ShapeDtypeStruct((2 * half_of(columns), depth), gate_t.dtype),
        scratch_shapes=[pltpu.SemaphoreType.DMA((2,))],
        compiler_params=pltpu.CompilerParams(vmem_limit_bytes=LARGE),
        cost_estimate=pl.CostEstimate(flops=0, bytes_accessed=4 * gate_t.size, transcendentals=0),
        name="cut",
    )(gate_t, up_t)


def pack_kernel(chunks, places, gate_ref, up_ref, got_ref, *refs):
    outs, sems = refs[:-1], refs[-1]
    _, core = line_position()
    columns, depth = gate_ref.shape
    half = half_of(columns)
    first = half_start(core, columns)

    def fill(me):
        copies = []
        for o, row, i in places:
            start, size = chunks[i]
            for k, w in enumerate((gate_ref, up_ref)):
                target = outs[o].at[pl.ds(row + k * size, size)]
                mine = target.at[:, pl.ds(me * depth, depth)]
                other = target.at[:, pl.ds((1 - me) * depth, depth)]
                sources = (w.at[pl.ds(first + start, size)], mine), (got_ref.at[pl.ds(k * half + start, size)], other)
                for source, target_part in sources:
                    copies.append(pltpu.make_async_copy(source, target_part, sems.at[len(copies)]))
        copy_all(copies)

    for me in range(CORES):
        pl.when(core == me)(functools.partial(fill, me))


def pack(gate_t, up_t, got, chunks, wanted):
    depth = gate_t.shape[1]
    in_hbm = pl.BlockSpec(memory_space=pltpu.HBM)
    whole = pl.BlockSpec(memory_space=pltpu.VMEM)
    places, out_shape = [], []
    for o, group in enumerate(wanted):
        row = 0
        for i in group:
            places.append((o, row, i))
            row += 2 * chunks[i][1]
        out_shape.append(jax.ShapeDtypeStruct((row, CORES * depth), gate_t.dtype))
    return pl.pallas_call(
        functools.partial(pack_kernel, chunks, places),
        in_specs=[in_hbm, in_hbm, whole],
        out_specs=[whole] * len(wanted),
        out_shape=out_shape,
        scratch_shapes=[pltpu.SemaphoreType.DMA((4 * len(places),))],
        compiler_params=pltpu.CompilerParams(vmem_limit_bytes=SMALL),
        cost_estimate=pl.CostEstimate(flops=0, bytes_accessed=8 * gate_t.size, transcendentals=0),
        name="pack",
    )(gate_t, up_t, got)


def turn_kernel(own_ref, outer_ref, out_ref):
    rows = own_ref.shape[0]
    out_ref[:, :rows] = own_ref[...].T
    out_ref[:, rows:] = outer_ref[...].T


def turn(own, outer):
    rows, features = own.shape
    return pl.pallas_call(
        turn_kernel,
        in_specs=[pl.BlockSpec(memory_space=pltpu.VMEM)] * 2,
        out_specs=pl.BlockSpec(memory_space=pltpu.VMEM),
        out_shape=jax.ShapeDtypeStruct((features, 2 * rows), own.dtype),
        compiler_params=pltpu.CompilerParams(vmem_limit_bytes=4 * SMALL),
        cost_estimate=pl.CostEstimate(flops=0, bytes_accessed=8 * own.size, transcendentals=0),
        name="turn",
    )(own, outer)


def arrange_kernel(*refs):
    blocks, out_ref, sems = refs[:LINE], refs[LINE], refs[LINE + 1]
    chip, _ = line_position()
    group = lax.axis_index("narrow")
    features = blocks[0].shape[0]
    copies = []
    for d, block in enumerate(blocks):
        want = chip ^ group ^ d
        place = jnp.where(want == TURN[1], 1, jnp.where(want == TURN[2], 2, jnp.where(want == TURN[3], 3, 0)))
        row = pl.multiple_of(place * features, features)
        copies.append(pltpu.make_async_copy(block, out_ref.at[pl.ds(row, features)], sems.at[d]))
    copy_all(copies)


def arrange(blocks):
    features, rows = blocks[0].shape
    whole = pl.BlockSpec(memory_space=pltpu.VMEM)
    return pl.pallas_call(
        arrange_kernel,
        in_specs=[whole] * LINE,
        out_specs=whole,
        out_shape=jax.ShapeDtypeStruct((LINE * features, rows), blocks[0].dtype),
        scratch_shapes=[pltpu.SemaphoreType.DMA((LINE,))],
        compiler_params=pltpu.CompilerParams(vmem_limit_bytes=SMALL),
        cost_estimate=pl.CostEstimate(flops=0, bytes_accessed=4 * LINE * blocks[0].size, transcendentals=0),
        name="arrange",
    )(*blocks)


def store(result_ref, parts, sems, at=0):
    _, core = line_position()
    columns = result_ref.shape[0]
    copies = []
    for k, (ref, others, start) in enumerate(parts):
        first = half_start(1 - core if others else core, columns) + start
        target = result_ref.at[pl.ds(first, ref.shape[0])]
        copies.append(pltpu.make_async_copy(ref, target, sems.at[at + k]))
    return copies


def chunk_kernel(plan, x_ref, y_ref, *refs):
    start, step, joint, swap_stores, back_start, weight_rows = plan
    weights, refs = refs[:LINE], refs[LINE:]
    own_buf, sems = refs[-2:]
    size, rows = own_buf.shape
    result_ref, swap_ref, *outers = refs[-5 if joint else -6 : -2]
    if joint:
        outers = outers[0].at[:, pl.ds(0, rows)], outers[0].at[:, pl.ds(rows, rows)]

    def swap_store(k):
        if swap_stores is None or swap_stores[k] is None:
            return []
        first, count = swap_stores[k]
        return store(result_ref, [(refs[0].at[pl.ds(0, count)], True, first)], sems, 1)

    @pl.when(jnp.logical_not(at_end()))
    def _():
        copies = swap_store(0)
        for copy in copies:
            copy.start()
        for j in range(0, size, step):
            sides = [
                jnp.concatenate([w[pl.ds(r + k * size + j, step), :] for w, r in zip(weights, weight_rows)], axis=1)
                for k in (0, 1)
            ]
            both_w = jnp.concatenate(sides, axis=0)
            here = pl.ds(j, step)
            for tokens_ref, own_out, outer_out in ((x_ref, own_buf, outers[0]), (y_ref, swap_ref, outers[1])):
                both = jnp.dot(both_w, tokens_ref[...], preferred_element_type=jnp.float32)
                hidden = gated(both[:step], both[step:])
                own_out[here, :] = hidden[:, :rows]
                outer_out[here, :] = hidden[:, rows:]
        copies += store(result_ref, [(own_buf, False, start)], sems)
        copies[-1].start()
        for copy in copies:
            copy.wait()

    if back_start is not None:
        back_ref = refs[1]

        @pl.when(at_end())
        def _():
            count = back_ref.shape[0]
            mine = back_ref.at[:, pl.ds(0, rows)]
            copies = store(result_ref, [(mine, False, back_start)], sems) + swap_store(1)
            copies.append(
                pltpu.make_async_copy(back_ref.at[:, pl.ds(rows, rows)], swap_ref.at[pl.ds(0, count)], sems.at[2])
            )
            copy_all(copies)


def chunk_hidden(x, y, weights, start, size, step, result, joint, swapped=None, back=None):
    rows = x.shape[1] // 2
    whole = pl.BlockSpec(memory_space=pltpu.VMEM)
    in_hbm = pl.BlockSpec(memory_space=pltpu.HBM)
    operands = [x, y] + [w for w, _ in weights]
    swap_rows = size
    if swapped is not None:
        operands.append(swapped[0])
    if back is not None:
        operands.append(back[0])
        swap_rows = max(size, back[0].shape[0])
    in_specs = [whole] * len(operands)
    aliases = {}
    if not isinstance(result, jax.ShapeDtypeStruct):
        aliases = {len(operands): 0}
        operands.append(result)
        in_specs.append(in_hbm)
    out_shape = [jax.ShapeDtypeStruct(result.shape, result.dtype), jax.ShapeDtypeStruct((swap_rows, rows), result.dtype)]
    out_shape += [jax.ShapeDtypeStruct((size, rows * (2 if joint else 1)), result.dtype)] * (1 if joint else 2)
    plan = (start, step, joint, swapped and swapped[1], back and back[1], [r for _, r in weights])
    return pl.pallas_call(
        functools.partial(chunk_kernel, plan),
        in_specs=in_specs,
        out_specs=[in_hbm] + [whole] * (len(out_shape) - 1),
        out_shape=out_shape,
        scratch_shapes=[pltpu.VMEM((size, rows), result.dtype), pltpu.SemaphoreType.DMA((3,))],
        input_output_aliases=aliases,
        compiler_params=pltpu.CompilerParams(vmem_limit_bytes=VMEM),
        cost_estimate=pl.CostEstimate(flops=0, bytes_accessed=2 * size * rows, transcendentals=0),
        name="chunk_hidden",
    )(*operands)


def put_kernel(stores, *refs):
    result_ref, sems = refs[-2:]
    for end in (0, 1):

        @pl.when(at_end() == (end == 1))
        def _():
            parts = [
                (refs[k].at[pl.ds(0, count)], others, first) for k, others, first, count in stores[end]
            ]
            copy_all(store(result_ref, parts, sems))


def put(result, arrays, stores):
    in_hbm = pl.BlockSpec(memory_space=pltpu.HBM)
    return pl.pallas_call(
        functools.partial(put_kernel, stores),
        in_specs=[pl.BlockSpec(memory_space=pltpu.VMEM)] * len(arrays) + [in_hbm],
        out_specs=in_hbm,
        out_shape=jax.ShapeDtypeStruct(result.shape, result.dtype),
        scratch_shapes=[pltpu.SemaphoreType.DMA((len(arrays),))],
        input_output_aliases={len(arrays): 0},
        compiler_params=pltpu.CompilerParams(vmem_limit_bytes=SMALL),
        cost_estimate=pl.CostEstimate(flops=0, bytes_accessed=4 * arrays[0].size, transcendentals=0),
        name="put",
    )(*arrays, result)


def after(x, *earlier):
    return lax.optimization_barrier((x, *earlier))[0]


def folded(tokens, gate_weight, up_weight):
    rows_own = tokens.shape[0]
    columns_dev = gate_weight.shape[1]

    def between(pairs, cross=0):
        return [(s * CORES + c, t * CORES + (c ^ cross)) for s, t in pairs for c in range(CORES)]

    inward = between([(0, 1), (3, 2)])
    outward = between([(1, 0), (2, 3)])
    outward_cross = between([(1, 0), (2, 3)], 1)
    across = between([(1, 2), (2, 1)])
    other_core = [(i, i ^ 1) for i in range(LINE * CORES)]

    def send(x, pairs):
        return lax.ppermute(x, "wide", pairs)

    tiles = half_of(columns_dev) // TILE
    counts = [tiles * p // 116 for p in SHARES]
    counts.append(tiles - sum(counts))
    h = [TILE * t for t in counts]
    starts = [sum(h[:i]) for i in range(3)]

    mine = gate_weight.T, up_weight.T
    outer_tokens = send(tokens, inward)
    got = after(send(cut(*mine), other_core), outer_tokens)
    chunks = list(zip(starts, h))
    pack_01, pack_0 = pack(*mine, got, chunks, ((0, 1), (0,)))
    pack_1, pack_2 = pack(*mine, got, chunks, ((1,), (2,)))

    own_01 = send(pack_01, across)
    outer_0 = send(pack_0, inward)
    outer_1 = send(pack_1, inward)
    outer_2 = send(after(pack_2, outer_0), inward)
    far_0 = send(outer_0, across)

    both = turn(after(tokens, pack_0), outer_tokens)
    blocks = [both] + [lax.ppermute(both, "narrow", [(i, i ^ d) for i in range(LINE)]) for d in (1, 2, 3)]
    x = arrange(blocks)
    y = send(x, other_core)

    far_1 = send(after(outer_1, own_01), across)
    own_2 = send(after(pack_2, far_0), across)
    far_2 = send(after(outer_2, far_1), across)
    second = 2 * h[0]
    weights = [
        [(pack_01, 0), (own_01, 0), (outer_0, 0), (far_0, 0)],
        [(pack_01, second), (own_01, second), (outer_1, 0), (far_1, 0)],
        [(pack_2, 0), (own_2, 0), (outer_2, 0), (far_2, 0)],
    ]

    def compute(i, result, joint, **options):
        step = h[i] if h[i] <= 384 else h[i] // 2
        return chunk_hidden(x, y, weights[i], starts[i], h[i], step, result, joint, **options)

    result = jax.ShapeDtypeStruct((columns_dev, rows_own), jnp.bfloat16)
    result, swap, out = compute(0, result, True)
    back_0 = send(out, outward)
    swapped_0 = send(swap, other_core)
    result, swap, same, cross = compute(1, result, False, swapped=(swapped_0, (chunks[0], None)))
    back_1 = send(same, outward), send(cross, outward_cross)
    swapped_1 = send(swap, other_core)
    result, swap, same, cross = compute(
        2, result, False, swapped=(swapped_1, (chunks[1], None)), back=(back_0, starts[0])
    )
    back_2 = send(same, outward), send(cross, outward_cross)
    swapped_2 = send(swap, other_core)
    stores = [(0, True, *chunks[2])], [(0, True, *chunks[0]), (1, False, *chunks[1]), (2, True, *chunks[1])]
    result = put(result, (swapped_2, *back_1), stores)
    return put(result, back_2, ([], [(0, False, *chunks[2]), (1, True, *chunks[2])])).T


def solution(mesh):
    in_specs = (P("wide", "narrow"), P("wide", "narrow"), P("wide", "narrow"))
    out_specs = P("wide", "narrow")
    local = folded if mesh.shape["wide"] == LINE * CORES else gathered_everywhere
    return jax.shard_map(local, mesh=mesh, in_specs=in_specs, out_specs=out_specs, check_vma=False)
```

time: 178 us -> 119 us (0.67)
  waiting for transfers between devices: 133 us -> 79.3 us
  starting transfers between devices: 0.04 us -> 33.4 us
  blocking collectives: 15.9 us -> 0 us
  matrix products: 15.1 us -> 0 us
  between operations: 13.4 us -> 0.26 us
  Pallas kernels: 0 us -> 5.96 us
    all_gather x2 -> x0, waiting for transfers between devices: 132 us -> none  [the longest x1 68.4 us: local(): up_full = lax.all_gather(up_weight, 'wide', axis=0, tiled=True)]
    ppermute x0 -> x22, waiting for transfers between devices: none -> 79.3 us  [the longest x19 70.4 us: send(): return lax.ppermute(x, 'wide', pairs)]
    ppermute x0 -> x22, starting transfers between devices: none -> 33.4 us  [the longest x19 29.9 us: send(): return lax.ppermute(x, 'wide', pairs)]
    all_gather x1 -> x0, blocking collectives: 15.9 us -> none  [local(): gathered = lax.all_gather(tokens, 'narrow', axis=1, tiled=True)]
    dot_general x2 -> x0, matrix products: 15.1 us -> none  [the longest x1 7.95 us: project_block(): up = jnp.dot(rows, up_full, preferred_element_type=jnp.float32)]
    pallas_call x0 -> x10, Pallas kernels: none -> 5.96 us  [the longest x1 2.26 us: cut(): pl.pallas_call(cut_kernel, in_specs=[in_hbm, in_hbm], out_specs=pl.BlockS...]
  transfers between devices with their start and end apart: 2 -> 22, of which waited for: 2 -> 12; matrix products, arithmetic and copies ran while one was open for 4% -> 0% of each run, Pallas kernels for 0% -> 2%
where the time goes in v1:
time: 119 us
  waiting for transfers between devices  79.3 us (67%)
  starting transfers between devices  33.4 us (28%)
  Pallas kernels  5.96 us (5%)
    ppermute x19, waiting for transfers between devices, send(): return lax.ppermute(x, 'wide', pairs)  70.4 us
    ppermute x19, starting transfers between devices, send(): return lax.ppermute(x, 'wide', pairs)  29.9 us
    ppermute x3, waiting for transfers between devices, folded(): lax.ppermute(both, 'narrow', [(i, i ^ d) for i in range(LINE)])  8.85 us
    ppermute x3, starting transfers between devices, folded(): lax.ppermute(both, 'narrow', [(i, i ^ d) for i in range(LINE)])  3.55 us
  transfers between devices with their start and end apart: 22, of which 12 were waited for; matrix products, arithmetic and copies ran while one was open for 0% of the time, Pallas kernels for 2%

profile of v1, /device:TPU:0, one launch (start us, length us, event | category | flops | bytes accessed | tf_op | source)
XLA Modules:
  0.0 118.9 jit_solution(9735479727122779191)
XLA Ops:
  0.0 0.0 copy-start.1
  0.0 0.0 copy-start
  0.0 0.0 copy-start.2
  0.0 2.3 %cut.1 = bf16[3712,128]{1,0:T(8,128)(2,1)} custom-call(bf16[3696,128]{1,0:T(8,128)(2,1)} %bitcast.3, bf16[3696,128]{1,0:T(8,128)(2,1)} %bitcast.6), custom_call_target="tpu_custom_call" | custom-call | bytes 1892352 | tf_op jit(solution)/shard_map/cut/pallas_call | solution.py:74
  2.3 0.6 collective-permute-start
  2.8 0.0 copy-done.2
  2.8 4.5 %collective-permute-start.1 = (bf16[256,256]{1,0:T(8,128)(2,1)S(1)}, bf16[256,256]{1,0:T(8,128)(2,1)S(1)}, u32[]{:S(2)}, u32[]{:S(2)}) collective-permute-start(bf16[256,256]{1,0:T(8,128)(2,1)S(1)} %copy-done.2), channel_id=1, source_target_pairs={{0,8},{4,12},{24,16},{28,20},{1,9},{5,13},{25,17},{29,21},{2,10},{... | collective-permute-start | bytes 393224 | tf_op jit(solution)/shard_map/ppermute | solution.py:321
  7.4 3.4 %collective-permute-done.1.outer_ref = bf16[256,256]{1,0:T(8,128)(2,1)S(1)} collective-permute-done((bf16[256,256]{1,0:T(8,128)(2,1)S(1)}, bf16[256,256]{1,0:T(8,128)(2,1)S(1)}, u32[]{:S(2)}, u32[]{:S(2)}) %collective-permute-start.1) | collective-permute-done | bytes 131104 | tf_op jit(solution)/shard_map/ppermute | solution.py:321
  10.7 0.0 collective-permute-done.got_ref
  10.7 0.0 copy-done.1
  10.7 0.0 copy-done
  10.7 0.5 pack.2
  11.3 0.8 collective-permute-start.11
  12.0 7.2 %collective-permute-start.6 = (bf16[1472,256]{1,0:T(8,128)(2,1)S(1)}, bf16[1472,256]{1,0:T(8,128)(2,1)S(1)}, u32[]{:S(2)}, u32[]{:S(2)}) collective-permute-start(bf16[1472,256]{1,0:T(8,128)(2,1)S(1)} %get-tuple-element.27), channel_id=1, source_target_pairs={{0,8},{4,12},{24,16},{28,20},{1,9},{5,13},{25,17},{29,21},{2,10},{... | collective-permute-start | bytes 2261000 | tf_op jit(solution)/shard_map/ppermute | solution.py:321
  19.2 0.1 turn.1.refs_0_
  19.3 2.5 %collective-permute-start.4 = (bf16[256,512]{1,0:T(8,128)(2,1)S(1)}, bf16[256,512]{1,0:T(8,128)(2,1)S(1)}, u32[]{:S(2)}, u32[]{:S(2)}) collective-permute-start(bf16[256,512]{1,0:T(8,128)(2,1)S(1)} %turn.1.refs_0_), channel_id=1, source_target_pairs={{0,3},{1,2},{2,1},{3,0},{4,7},{5,6},{6,5},{7,4},{8,11},{9,10},{10,... | collective-permute-start | bytes 786440 | tf_op jit(solution)/shard_map/ppermute | solution.py:343
  21.9 0.5 collective-permute-start.3
  22.4 0.5 collective-permute-start.2
  22.9 0.3 pack.3
  23.2 6.4 %collective-permute-done.4.refs_3_ = bf16[256,512]{1,0:T(8,128)(2,1)S(1)} collective-permute-done((bf16[256,512]{1,0:T(8,128)(2,1)S(1)}, bf16[256,512]{1,0:T(8,128)(2,1)S(1)}, u32[]{:S(2)}, u32[]{:S(2)}) %collective-permute-start.4) | collective-permute-done | bytes 262176 | tf_op jit(solution)/shard_map/ppermute | solution.py:343
  29.6 1.3 %collective-permute-start.10 = (bf16[1472,256]{1,0:T(8,128)(2,1)S(1)}, bf16[1472,256]{1,0:T(8,128)(2,1)S(1)}, u32[]{:S(2)}, u32[]{:S(2)}) collective-permute-start(bf16[1472,256]{1,0:T(8,128)(2,1)S(1)} %get-tuple-element.32), channel_id=1, source_target_pairs={{0,8},{4,12},{24,16},{28,20},{1,9},{5,13},{25,17},{29,21},{2,10},{... | collective-permute-start | bytes 2261000 | tf_op jit(solution)/shard_map/ppermute | solution.py:321
  30.9 2.3 %collective-permute-done.3.refs_2_ = bf16[256,512]{1,0:T(8,128)(2,1)S(1)} collective-permute-done((bf16[256,512]{1,0:T(8,128)(2,1)S(1)}, bf16[256,512]{1,0:T(8,128)(2,1)S(1)}, u32[]{:S(2)}, u32[]{:S(2)}) %collective-permute-start.3) | collective-permute-done | bytes 262176 | tf_op jit(solution)/shard_map/ppermute | solution.py:343
  33.3 0.1 collective-permute-done.2.refs_1_
  33.4 0.1 arrange.1.x_ref
  33.5 0.1 collective-permute-start.5
  33.6 2.9 %collective-permute-done.6.refs_2_ = bf16[1472,256]{1,0:T(8,128)(2,1)S(1)} collective-permute-done((bf16[1472,256]{1,0:T(8,128)(2,1)S(1)}, bf16[1472,256]{1,0:T(8,128)(2,1)S(1)}, u32[]{:S(2)}, u32[]{:S(2)}) %collective-permute-start.6) | collective-permute-done | bytes 753696 | tf_op jit(solution)/shard_map/ppermute | solution.py:321
  36.5 0.7 collective-permute-start.7
  37.2 13.8 %collective-permute-done.10.refs_2_ = bf16[1472,256]{1,0:T(8,128)(2,1)S(1)} collective-permute-done((bf16[1472,256]{1,0:T(8,128)(2,1)S(1)}, bf16[1472,256]{1,0:T(8,128)(2,1)S(1)}, u32[]{:S(2)}, u32[]{:S(2)}) %collective-permute-start.10) | collective-permute-done | bytes 753696 | tf_op jit(solution)/shard_map/ppermute | solution.py:321
  51.0 0.0 collective-permute-done.11.refs_1_
  51.0 0.7 collective-permute-start.12
  51.7 6.1 %collective-permute-start.9 = (bf16[768,256]{1,0:T(8,128)(2,1)S(1)}, bf16[768,256]{1,0:T(8,128)(2,1)S(1)}, u32[]{:S(2)}, u32[]{:S(2)}) collective-permute-start(bf16[768,256]{1,0:T(8,128)(2,1)S(1)} %get-tuple-element.31.refs_0_), channel_id=1, source_target_pairs={{0,8},{4,12},{24,16},{28,20},{1,9},{5,13},{25,17},{29,21},{2,10},{... | collective-permute-start | bytes 1179656 | tf_op jit(solution)/shard_map/ppermute | solution.py:321
  57.8 0.0 collective-permute-done.5.y_ref
  57.8 0.0 collective-permute-done.7.refs_3_
  57.8 0.1 chunk_hidden.3
  57.8 0.1 collective-permute-start.14
  57.9 1.3 %collective-permute-start.16 = (bf16[736,512]{1,0:T(8,128)(2,1)S(1)}, bf16[736,512]{1,0:T(8,128)(2,1)S(1)}, u32[]{:S(2)}, u32[]{:S(2)}) collective-permute-start(bf16[736,512]{1,0:T(8,128)(2,1)S(1)} %get-tuple-element.39), channel_id=1, source_target_pairs={{8,0},{12,4},{16,24},{20,28},{9,1},{13,5},{17,25},{21,29},{10,2},{... | collective-permute-start | bytes 2261000 | tf_op jit(solution)/shard_map/ppermute | solution.py:321
  59.2 0.7 collective-permute-start.8
  59.9 4.6 %collective-permute-done.9.refs_2_ = bf16[768,256]{1,0:T(8,128)(2,1)S(1)} collective-permute-done((bf16[768,256]{1,0:T(8,128)(2,1)S(1)}, bf16[768,256]{1,0:T(8,128)(2,1)S(1)}, u32[]{:S(2)}, u32[]{:S(2)}) %collective-permute-start.9) | collective-permute-done | bytes 393248 | tf_op jit(solution)/shard_map/ppermute | solution.py:321
  64.5 0.0 collective-permute-done.12.refs_3_
  64.5 0.7 collective-permute-start.13
  65.2 0.0 collective-permute-done.14.refs_4_
  65.2 0.1 chunk_hidden.4
  65.2 0.1 collective-permute-start.15
  65.3 1.3 %collective-permute-start.20 = (bf16[736,256]{1,0:T(8,128)(2,1)S(1)}, bf16[736,256]{1,0:T(8,128)(2,1)S(1)}, u32[]{:S(2)}, u32[]{:S(2)}) collective-permute-start(bf16[736,256]{1,0:T(8,128)(2,1)S(1)} %get-tuple-element.44), channel_id=1, source_target_pairs={{8,0},{12,4},{16,24},{20,28},{9,1},{13,5},{17,25},{21,29},{10,2},{... | collective-permute-start | bytes 1130504 | tf_op jit(solution)/shard_map/ppermute | solution.py:321
  66.6 0.0 collective-permute-done.8.refs_1_
  66.6 1.3 %collective-permute-start.21 = (bf16[736,256]{1,0:T(8,128)(2,1)S(1)}, bf16[736,256]{1,0:T(8,128)(2,1)S(1)}, u32[]{:S(2)}, u32[]{:S(2)}) collective-permute-start(bf16[736,256]{1,0:T(8,128)(2,1)S(1)} %get-tuple-element.45), channel_id=1, source_target_pairs={{8,4},{12,0},{16,28},{20,24},{9,5},{13,1},{17,29},{21,25},{10,6},{... | collective-permute-start | bytes 1130504 | tf_op jit(solution)/shard_map/ppermute | solution.py:321
  67.9 22.3 %collective-permute-done.16.refs_5_ = bf16[736,512]{1,0:T(8,128)(2,1)S(1)} collective-permute-done((bf16[736,512]{1,0:T(8,128)(2,1)S(1)}, bf16[736,512]{1,0:T(8,128)(2,1)S(1)}, u32[]{:S(2)}, u32[]{:S(2)}) %collective-permute-start.16) | collective-permute-done | bytes 753696 | tf_op jit(solution)/shard_map/ppermute | solution.py:321
  90.2 0.0 collective-permute-done.15.refs_4_
  90.2 0.0 collective-permute-done.13.refs_3_
  90.2 0.8 chunk_hidden.5
  91.0 0.1 collective-permute-start.19
  91.0 1.3 %collective-permute-start.17 = (bf16[384,256]{1,0:T(8,128)(2,1)S(1)}, bf16[384,256]{1,0:T(8,128)(2,1)S(1)}, u32[]{:S(2)}, u32[]{:S(2)}) collective-permute-start(bf16[384,256]{1,0:T(8,128)(2,1)S(1)} %get-tuple-element.41), channel_id=1, source_target_pairs={{8,0},{12,4},{16,24},{20,28},{9,1},{13,5},{17,25},{21,29},{10,2},{... | collective-permute-start | bytes 589832 | tf_op jit(solution)/shard_map/ppermute | solution.py:321
  92.3 1.3 %collective-permute-start.18 = (bf16[384,256]{1,0:T(8,128)(2,1)S(1)}, bf16[384,256]{1,0:T(8,128)(2,1)S(1)}, u32[]{:S(2)}, u32[]{:S(2)}) collective-permute-start(bf16[384,256]{1,0:T(8,128)(2,1)S(1)} %get-tuple-element.42), channel_id=1, source_target_pairs={{8,4},{12,0},{16,28},{20,24},{9,5},{13,1},{17,29},{21,25},{10,6},{... | collective-permute-start | bytes 589832 | tf_op jit(solution)/shard_map/ppermute | solution.py:321
  93.6 8.4 %collective-permute-done.20.refs_1_ = bf16[736,256]{1,0:T(8,128)(2,1)S(1)} collective-permute-done((bf16[736,256]{1,0:T(8,128)(2,1)S(1)}, bf16[736,256]{1,0:T(8,128)(2,1)S(1)}, u32[]{:S(2)}, u32[]{:S(2)}) %collective-permute-start.20) | collective-permute-done | bytes 376864 | tf_op jit(solution)/shard_map/ppermute | solution.py:321
  102.1 7.7 %collective-permute-done.21.refs_2_ = bf16[736,256]{1,0:T(8,128)(2,1)S(1)} collective-permute-done((bf16[736,256]{1,0:T(8,128)(2,1)S(1)}, bf16[736,256]{1,0:T(8,128)(2,1)S(1)}, u32[]{:S(2)}, u32[]{:S(2)}) %collective-permute-start.21) | collective-permute-done | bytes 376864 | tf_op jit(solution)/shard_map/ppermute | solution.py:321
  109.7 0.0 collective-permute-done.19.refs_0_
  109.7 1.0 put.2.refs_2_
  110.8 3.6 %collective-permute-done.17.refs_0_ = bf16[384,256]{1,0:T(8,128)(2,1)S(1)} collective-permute-done((bf16[384,256]{1,0:T(8,128)(2,1)S(1)}, bf16[384,256]{1,0:T(8,128)(2,1)S(1)}, u32[]{:S(2)}, u32[]{:S(2)}) %collective-permute-start.17) | collective-permute-done | bytes 196640 | tf_op jit(solution)/shard_map/ppermute | solution.py:321
  114.4 3.8 %collective-permute-done.18.refs_1_ = bf16[384,256]{1,0:T(8,128)(2,1)S(1)} collective-permute-done((bf16[384,256]{1,0:T(8,128)(2,1)S(1)}, bf16[384,256]{1,0:T(8,128)(2,1)S(1)}, u32[]{:S(2)}, u32[]{:S(2)}) %collective-permute-start.18) | collective-permute-done | bytes 196640 | tf_op jit(solution)/shard_map/ppermute | solution.py:321
  118.2 0.8 put.3
Async XLA Ops:
  0.0 10.7 %copy-start.1 = (bf16[128,3696]{0,1:T(8,128)(2,1)S(1)}, bf16[128,3696]{0,1:T(8,128)(2,1)}, u32[]{:S(2)}) copy-start(bf16[128,3696]{0,1:T(8,128)(2,1)} %param.5) | copy-start | bytes 2838532
  0.0 10.7 %copy-start = (bf16[128,3696]{0,1:T(8,128)(2,1)S(1)}, bf16[128,3696]{0,1:T(8,128)(2,1)}, u32[]{:S(2)}) copy-start(bf16[128,3696]{0,1:T(8,128)(2,1)} %param.4) | copy-start | bytes 2838532
  0.0 2.8 %copy-start.2 = (bf16[256,256]{1,0:T(8,128)(2,1)S(1)}, bf16[256,256]{1,0:T(8,128)(2,1)}, u32[]{:S(2)}) copy-start(bf16[256,256]{1,0:T(8,128)(2,1)} %own_ref) | copy-start | bytes 393220
  2.3 8.5 %collective-permute-start = (bf16[3712,128]{1,0:T(8,128)(2,1)}, bf16[3712,128]{1,0:T(8,128)(2,1)S(1)}, u32[]{:S(2)}, u32[]{:S(2)}) collective-permute-start(bf16[3712,128]{1,0:T(8,128)(2,1)} %cut.1), channel_id=1, source_target_pairs={{0,4},{4,0},{8,12},{12,8},{16,20},{20,16},{24,28},{28,24},{1,5},{5... | collective-permute-start | bytes 2850824 | tf_op jit(solution)/shard_map/ppermute | solution.py:321
  2.8 7.9 %collective-permute-start.1 = (bf16[256,256]{1,0:T(8,128)(2,1)S(1)}, bf16[256,256]{1,0:T(8,128)(2,1)S(1)}, u32[]{:S(2)}, u32[]{:S(2)}) collective-permute-start(bf16[256,256]{1,0:T(8,128)(2,1)S(1)} %copy-done.2), channel_id=1, source_target_pairs={{0,8},{4,12},{24,16},{28,20},{1,9},{5,13},{25,17},{29,21},{2,10},{... | collective-permute-start | bytes 393224 | tf_op jit(solution)/shard_map/ppermute | solution.py:321
  11.3 39.7 %collective-permute-start.11 = (bf16[2944,256]{1,0:T(8,128)(2,1)S(1)}, bf16[2944,256]{1,0:T(8,128)(2,1)S(1)}, u32[]{:S(2)}, u32[]{:S(2)}) collective-permute-start(bf16[2944,256]{1,0:T(8,128)(2,1)S(1)} %get-tuple-element.33.refs_0_), channel_id=1, source_target_pairs={{8,16},{12,20},{16,8},{20,12},{9,17},{13,21},{17,9},{21,13},{10,18... | collective-permute-start | bytes 4521992 | tf_op jit(solution)/shard_map/ppermute | solution.py:321
  12.0 24.4 %collective-permute-start.6 = (bf16[1472,256]{1,0:T(8,128)(2,1)S(1)}, bf16[1472,256]{1,0:T(8,128)(2,1)S(1)}, u32[]{:S(2)}, u32[]{:S(2)}) collective-permute-start(bf16[1472,256]{1,0:T(8,128)(2,1)S(1)} %get-tuple-element.27), channel_id=1, source_target_pairs={{0,8},{4,12},{24,16},{28,20},{1,9},{5,13},{25,17},{29,21},{2,10},{... | collective-permute-start | bytes 2261000 | tf_op jit(solution)/shard_map/ppermute | solution.py:321
  19.3 10.3 %collective-permute-start.4 = (bf16[256,512]{1,0:T(8,128)(2,1)S(1)}, bf16[256,512]{1,0:T(8,128)(2,1)S(1)}, u32[]{:S(2)}, u32[]{:S(2)}) collective-permute-start(bf16[256,512]{1,0:T(8,128)(2,1)S(1)} %turn.1.refs_0_), channel_id=1, source_target_pairs={{0,3},{1,2},{2,1},{3,0},{4,7},{5,6},{6,5},{7,4},{8,11},{9,10},{10,... | collective-permute-start | bytes 786440 | tf_op jit(solution)/shard_map/ppermute | solution.py:343
  21.9 11.4 %collective-permute-start.3 = (bf16[256,512]{1,0:T(8,128)(2,1)S(1)}, bf16[256,512]{1,0:T(8,128)(2,1)S(1)}, u32[]{:S(2)}, u32[]{:S(2)}) collective-permute-start(bf16[256,512]{1,0:T(8,128)(2,1)S(1)} %turn.1.refs_0_), channel_id=1, source_target_pairs={{0,2},{1,3},{2,0},{3,1},{4,6},{5,7},{6,4},{7,5},{8,10},{9,11},{10,... | collective-permute-start | bytes 786440 | tf_op jit(solution)/shard_map/ppermute | solution.py:343
  22.4 11.0 %collective-permute-start.2 = (bf16[256,512]{1,0:T(8,128)(2,1)S(1)}, bf16[256,512]{1,0:T(8,128)(2,1)S(1)}, u32[]{:S(2)}, u32[]{:S(2)}) collective-permute-start(bf16[256,512]{1,0:T(8,128)(2,1)S(1)} %turn.1.refs_0_), channel_id=1, source_target_pairs={{0,1},{1,0},{2,3},{3,2},{4,5},{5,4},{6,7},{7,6},{8,9},{9,8},{10,11... | collective-permute-start | bytes 786440 | tf_op jit(solution)/shard_map/ppermute | solution.py:343
  29.6 21.4 %collective-permute-start.10 = (bf16[1472,256]{1,0:T(8,128)(2,1)S(1)}, bf16[1472,256]{1,0:T(8,128)(2,1)S(1)}, u32[]{:S(2)}, u32[]{:S(2)}) collective-permute-start(bf16[1472,256]{1,0:T(8,128)(2,1)S(1)} %get-tuple-element.32), channel_id=1, source_target_pairs={{0,8},{4,12},{24,16},{28,20},{1,9},{5,13},{25,17},{29,21},{2,10},{... | collective-permute-start | bytes 2261000 | tf_op jit(solution)/shard_map/ppermute | solution.py:321
  33.5 24.3 %collective-permute-start.5 = (bf16[1024,512]{1,0:T(8,128)(2,1)S(1)}, bf16[1024,512]{1,0:T(8,128)(2,1)S(1)}, u32[]{:S(2)}, u32[]{:S(2)}) collective-permute-start(bf16[1024,512]{1,0:T(8,128)(2,1)S(1)} %arrange.1.x_ref), channel_id=1, source_target_pairs={{0,4},{4,0},{8,12},{12,8},{16,20},{20,16},{24,28},{28,24},{1,5},{5... | collective-permute-start | bytes 3145736 | tf_op jit(solution)/shard_map/ppermute | solution.py:321
  36.5 21.3 %collective-permute-start.7 = (bf16[1472,256]{1,0:T(8,128)(2,1)S(1)}, bf16[1472,256]{1,0:T(8,128)(2,1)S(1)}, u32[]{:S(2)}, u32[]{:S(2)}) collective-permute-start(bf16[1472,256]{1,0:T(8,128)(2,1)S(1)} %collective-permute-done.6.refs_2_), channel_id=1, source_target_pairs={{8,16},{12,20},{16,8},{20,12},{9,17},{13,21},{17,9},{21,13},{10,18... | collective-permute-start | bytes 2261000 | tf_op jit(solution)/shard_map/ppermute | solution.py:321
  51.0 13.5 %collective-permute-start.12 = (bf16[1472,256]{1,0:T(8,128)(2,1)S(1)}, bf16[1472,256]{1,0:T(8,128)(2,1)S(1)}, u32[]{:S(2)}, u32[]{:S(2)}) collective-permute-start(bf16[1472,256]{1,0:T(8,128)(2,1)S(1)} %collective-permute-done.10.refs_2_), channel_id=1, source_target_pairs={{8,16},{12,20},{16,8},{20,12},{9,17},{13,21},{17,9},{21,13},{10,18... | collective-permute-start | bytes 2261000 | tf_op jit(solution)/shard_map/ppermute | solution.py:321
  51.7 12.8 %collective-permute-start.9 = (bf16[768,256]{1,0:T(8,128)(2,1)S(1)}, bf16[768,256]{1,0:T(8,128)(2,1)S(1)}, u32[]{:S(2)}, u32[]{:S(2)}) collective-permute-start(bf16[768,256]{1,0:T(8,128)(2,1)S(1)} %get-tuple-element.31.refs_0_), channel_id=1, source_target_pairs={{0,8},{4,12},{24,16},{28,20},{1,9},{5,13},{25,17},{29,21},{2,10},{... | collective-permute-start | bytes 1179656 | tf_op jit(solution)/shard_map/ppermute | solution.py:321
  57.8 7.3 %collective-permute-start.14 = (bf16[736,256]{1,0:T(8,128)(2,1)S(1)}, bf16[736,256]{1,0:T(8,128)(2,1)S(1)}, u32[]{:S(2)}, u32[]{:S(2)}) collective-permute-start(bf16[736,256]{1,0:T(8,128)(2,1)S(1)} %get-tuple-element.36), channel_id=1, source_target_pairs={{0,4},{4,0},{8,12},{12,8},{16,20},{20,16},{24,28},{28,24},{1,5},{5... | collective-permute-start | bytes 1130504 | tf_op jit(solution)/shard_map/ppermute | solution.py:321
  57.9 32.3 %collective-permute-start.16 = (bf16[736,512]{1,0:T(8,128)(2,1)S(1)}, bf16[736,512]{1,0:T(8,128)(2,1)S(1)}, u32[]{:S(2)}, u32[]{:S(2)}) collective-permute-start(bf16[736,512]{1,0:T(8,128)(2,1)S(1)} %get-tuple-element.39), channel_id=1, source_target_pairs={{8,0},{12,4},{16,24},{20,28},{9,1},{13,5},{17,25},{21,29},{10,2},{... | collective-permute-start | bytes 2261000 | tf_op jit(solution)/shard_map/ppermute | solution.py:321
  59.2 7.4 %collective-permute-start.8 = (bf16[768,256]{1,0:T(8,128)(2,1)S(1)}, bf16[768,256]{1,0:T(8,128)(2,1)S(1)}, u32[]{:S(2)}, u32[]{:S(2)}) collective-permute-start(bf16[768,256]{1,0:T(8,128)(2,1)S(1)} %get-tuple-element.31.refs_0_), channel_id=1, source_target_pairs={{8,16},{12,20},{16,8},{20,12},{9,17},{13,21},{17,9},{21,13},{10,18... | collective-permute-start | bytes 1179656 | tf_op jit(solution)/shard_map/ppermute | solution.py:321
  64.5 25.7 %collective-permute-start.13 = (bf16[768,256]{1,0:T(8,128)(2,1)S(1)}, bf16[768,256]{1,0:T(8,128)(2,1)S(1)}, u32[]{:S(2)}, u32[]{:S(2)}) collective-permute-start(bf16[768,256]{1,0:T(8,128)(2,1)S(1)} %collective-permute-done.9.refs_2_), channel_id=1, source_target_pairs={{8,16},{12,20},{16,8},{20,12},{9,17},{13,21},{17,9},{21,13},{10,18... | collective-permute-start | bytes 1179656 | tf_op jit(solution)/shard_map/ppermute | solution.py:321
  65.2 25.0 %collective-permute-start.15 = (bf16[736,256]{1,0:T(8,128)(2,1)S(1)}, bf16[736,256]{1,0:T(8,128)(2,1)S(1)}, u32[]{:S(2)}, u32[]{:S(2)}) collective-permute-start(bf16[736,256]{1,0:T(8,128)(2,1)S(1)} %get-tuple-element.38), channel_id=1, source_target_pairs={{0,4},{4,0},{8,12},{12,8},{16,20},{20,16},{24,28},{28,24},{1,5},{5... | collective-permute-start | bytes 1130504 | tf_op jit(solution)/shard_map/ppermute | solution.py:321
  65.3 36.8 %collective-permute-start.20 = (bf16[736,256]{1,0:T(8,128)(2,1)S(1)}, bf16[736,256]{1,0:T(8,128)(2,1)S(1)}, u32[]{:S(2)}, u32[]{:S(2)}) collective-permute-start(bf16[736,256]{1,0:T(8,128)(2,1)S(1)} %get-tuple-element.44), channel_id=1, source_target_pairs={{8,0},{12,4},{16,24},{20,28},{9,1},{13,5},{17,25},{21,29},{10,2},{... | collective-permute-start | bytes 1130504 | tf_op jit(solution)/shard_map/ppermute | solution.py:321
  66.6 43.1 %collective-permute-start.21 = (bf16[736,256]{1,0:T(8,128)(2,1)S(1)}, bf16[736,256]{1,0:T(8,128)(2,1)S(1)}, u32[]{:S(2)}, u32[]{:S(2)}) collective-permute-start(bf16[736,256]{1,0:T(8,128)(2,1)S(1)} %get-tuple-element.45), channel_id=1, source_target_pairs={{8,4},{12,0},{16,28},{20,24},{9,5},{13,1},{17,29},{21,25},{10,6},{... | collective-permute-start | bytes 1130504 | tf_op jit(solution)/shard_map/ppermute | solution.py:321
  91.0 18.8 %collective-permute-start.19 = (bf16[736,256]{1,0:T(8,128)(2,1)S(1)}, bf16[736,256]{1,0:T(8,128)(2,1)S(1)}, u32[]{:S(2)}, u32[]{:S(2)}) collective-permute-start(bf16[736,256]{1,0:T(8,128)(2,1)S(1)} %get-tuple-element.43), channel_id=1, source_target_pairs={{0,4},{4,0},{8,12},{12,8},{16,20},{20,16},{24,28},{28,24},{1,5},{5... | collective-permute-start | bytes 1130504 | tf_op jit(solution)/shard_map/ppermute | solution.py:321
  91.0 23.3 %collective-permute-start.17 = (bf16[384,256]{1,0:T(8,128)(2,1)S(1)}, bf16[384,256]{1,0:T(8,128)(2,1)S(1)}, u32[]{:S(2)}, u32[]{:S(2)}) collective-permute-start(bf16[384,256]{1,0:T(8,128)(2,1)S(1)} %get-tuple-element.41), channel_id=1, source_target_pairs={{8,0},{12,4},{16,24},{20,28},{9,1},{13,5},{17,25},{21,29},{10,2},{... | collective-permute-start | bytes 589832 | tf_op jit(solution)/shard_map/ppermute | solution.py:321
  92.3 25.8 %collective-permute-start.18 = (bf16[384,256]{1,0:T(8,128)(2,1)S(1)}, bf16[384,256]{1,0:T(8,128)(2,1)S(1)}, u32[]{:S(2)}, u32[]{:S(2)}) collective-permute-start(bf16[384,256]{1,0:T(8,128)(2,1)S(1)} %get-tuple-element.42), channel_id=1, source_target_pairs={{8,4},{12,0},{16,28},{20,24},{9,5},{13,1},{17,29},{21,25},{10,6},{... | collective-permute-start | bytes 589832 | tf_op jit(solution)/shard_map/ppermute | solution.py:321

commit v2 on v1

v2 whole, which is shorter than its diff:
```python
import functools

import jax
import jax.numpy as jnp
from jax import lax
from jax.experimental import pallas as pl
from jax.experimental.pallas import tpu as pltpu
from jax.sharding import PartitionSpec as P

CORES = 2
LINE = 4
TILE = 16
SHARES = (44, 46)
TURN = (0, 3, 1, 2)
VMEM = 24 * 1024 * 1024
SMALL = 1024 * 1024
LARGE = 56 * 1024 * 1024


def gated(gate, up):
    return (jax.nn.silu(gate) * up).astype(jnp.bfloat16)


def gathered_everywhere(tokens, gate_weight, up_weight):
    rows = lax.all_gather(tokens, "narrow", axis=1, tiled=True)
    gate_full = lax.all_gather(gate_weight, "wide", axis=0, tiled=True)
    up_full = lax.all_gather(up_weight, "wide", axis=0, tiled=True)
    gate = jnp.dot(rows, gate_full, preferred_element_type=jnp.float32)
    up = jnp.dot(rows, up_full, preferred_element_type=jnp.float32)
    return gated(gate, up)


def line_position():
    index = lax.axis_index("wide")
    return index // CORES, index % CORES


def at_end():
    chip, _ = line_position()
    return (chip == 0) | (chip == LINE - 1)


def half_start(core, columns):
    return pl.multiple_of(core * (columns - half_of(columns)), TILE)


def half_of(columns):
    return -(-columns // (CORES * TILE)) * TILE


def copy_all(copies):
    for copy in copies:
        copy.start()
    for copy in copies:
        copy.wait()


def strips(size):
    strip = -(-size // (4 * TILE)) * TILE
    return [(at, min(strip, size - at)) for at in range(0, size, strip)]


def cut_kernel(start, size, gate_ref, up_ref, out_ref, sems):
    _, core = line_position()
    theirs = half_start(1 - core, gate_ref.shape[0]) + start
    copies = []
    for k, w in enumerate((gate_ref, up_ref)):
        for at, count in strips(size):
            target = out_ref.at[pl.ds(k * size + at, count)]
            copies.append(pltpu.make_async_copy(w.at[pl.ds(theirs + at, count)], target, sems.at[len(copies)]))
    copy_all(copies)


def cut(gate_t, up_t, start, size, room):
    in_hbm = pl.BlockSpec(memory_space=pltpu.HBM)
    return pl.pallas_call(
        functools.partial(cut_kernel, start, size),
        in_specs=[in_hbm, in_hbm],
        out_specs=pl.BlockSpec(memory_space=pltpu.VMEM),
        out_shape=jax.ShapeDtypeStruct((2 * size, gate_t.shape[1]), gate_t.dtype),
        scratch_shapes=[pltpu.SemaphoreType.DMA((8,))],
        compiler_params=pltpu.CompilerParams(vmem_limit_bytes=room),
        cost_estimate=pl.CostEstimate(flops=0, bytes_accessed=4 * gate_t.size, transcendentals=0),
        name="cut",
    )(gate_t, up_t)


def pack_kernel(chunks, got_start, places, gate_ref, up_ref, got_ref, *refs):
    outs, sems = refs[:-1], refs[-1]
    _, core = line_position()
    columns, depth = gate_ref.shape
    got_size = got_ref.shape[0] // 2
    first = half_start(core, columns)

    def fill(me):
        copies = []
        for o, row, i in places:
            start, size = chunks[i]
            for k, w in enumerate((gate_ref, up_ref)):
                target = outs[o].at[pl.ds(row + k * size, size)]
                mine = target.at[:, pl.ds(me * depth, depth)]
                other = target.at[:, pl.ds((1 - me) * depth, depth)]
                sources = (w.at[pl.ds(first + start, size)], mine), (
                    got_ref.at[pl.ds(k * got_size + start - got_start, size)],
                    other,
                )
                for source, target_part in sources:
                    copies.append(pltpu.make_async_copy(source, target_part, sems.at[len(copies)]))
        copy_all(copies)

    for me in range(CORES):
        pl.when(core == me)(functools.partial(fill, me))


def pack(gate_t, up_t, got, got_start, chunks, wanted):
    depth = gate_t.shape[1]
    in_hbm = pl.BlockSpec(memory_space=pltpu.HBM)
    whole = pl.BlockSpec(memory_space=pltpu.VMEM)
    places, out_shape = [], []
    for o, group in enumerate(wanted):
        row = 0
        for i in group:
            places.append((o, row, i))
            row += 2 * chunks[i][1]
        out_shape.append(jax.ShapeDtypeStruct((row, CORES * depth), gate_t.dtype))
    return pl.pallas_call(
        functools.partial(pack_kernel, chunks, got_start, places),
        in_specs=[in_hbm, in_hbm, whole],
        out_specs=[whole] * len(wanted),
        out_shape=out_shape,
        scratch_shapes=[pltpu.SemaphoreType.DMA((4 * len(places),))],
        compiler_params=pltpu.CompilerParams(vmem_limit_bytes=SMALL),
        cost_estimate=pl.CostEstimate(flops=0, bytes_accessed=8 * gate_t.size, transcendentals=0),
        name="pack",
    )(gate_t, up_t, got)


def arrange_kernel(*refs):
    blocks, outs = refs[:LINE], refs[LINE:]
    chip, _ = line_position()
    group = lax.axis_index("narrow")
    features = blocks[0].shape[1]
    for d, block in enumerate(blocks):
        turned = block[...].T
        for out, at in zip(outs, (chip, chip ^ 1)):
            want = at ^ group ^ d
            place = jnp.where(want == TURN[1], 1, jnp.where(want == TURN[2], 2, jnp.where(want == TURN[3], 3, 0)))
            out[pl.ds(pl.multiple_of(place * features, features), features), :] = turned


def arrange(blocks):
    rows, features = blocks[0].shape
    whole = pl.BlockSpec(memory_space=pltpu.VMEM)
    return pl.pallas_call(
        arrange_kernel,
        in_specs=[whole] * LINE,
        out_specs=[whole] * 2,
        out_shape=[jax.ShapeDtypeStruct((LINE * features, rows), blocks[0].dtype)] * 2,
        compiler_params=pltpu.CompilerParams(vmem_limit_bytes=4 * SMALL),
        cost_estimate=pl.CostEstimate(flops=0, bytes_accessed=4 * LINE * blocks[0].size, transcendentals=0),
        name="arrange",
    )(*blocks)


def store(result_ref, parts, sems, at=0):
    _, core = line_position()
    columns = result_ref.shape[0]
    copies = []
    for k, (ref, others, start) in enumerate(parts):
        first = half_start(1 - core if others else core, columns) + start
        target = result_ref.at[pl.ds(first, ref.shape[0])]
        copies.append(pltpu.make_async_copy(ref, target, sems.at[at + k]))
    return copies


def products(blocks, weights, tokens, outs):
    for j, step, sources in blocks:
        sides = [
            jnp.concatenate([weights[source[0]][pl.ds(source[k], step), :] for source in sources], axis=1)
            for k in (1, 2)
        ]
        both_w = jnp.concatenate(sides, axis=0)
        for tokens_ref, out in zip(tokens, outs):
            both = jnp.dot(both_w, tokens_ref[...], preferred_element_type=jnp.float32)
            out[pl.ds(j, step), :] = gated(both[:step], both[step:])


def outer_kernel(blocks, count, *refs):
    tokens, weights, outs = refs[:2], refs[2 : 2 + count], refs[2 + count :]
    rows = tokens[0].shape[1]
    if len(outs) == 1:
        outs = outs[0].at[:, pl.ds(0, rows)], outs[0].at[:, pl.ds(rows, rows)]
    pl.when(jnp.logical_not(at_end()))(functools.partial(products, blocks, weights, tokens, outs))


def outer_hidden(tokens, weights, blocks, size, joint):
    features, rows = tokens[0].shape
    whole = pl.BlockSpec(memory_space=pltpu.VMEM)
    return pl.pallas_call(
        functools.partial(outer_kernel, blocks, len(weights)),
        in_specs=[whole] * (2 + len(weights)),
        out_specs=[whole] * (1 if joint else 2),
        out_shape=[jax.ShapeDtypeStruct((size, rows * (2 if joint else 1)), tokens[0].dtype)] * (1 if joint else 2),
        compiler_params=pltpu.CompilerParams(vmem_limit_bytes=VMEM),
        cost_estimate=pl.CostEstimate(flops=0, bytes_accessed=2 * size * rows, transcendentals=0),
        name="outer_hidden",
    )(*tokens, *weights)


def own_kernel(plan, *refs):
    start, blocks, swap_stores, back_start, count = plan
    tokens, weights, refs = refs[:2], refs[2 : 2 + count], refs[2 + count :]
    result_ref, swap_ref, own_buf, sems = refs[-4:]
    rows = own_buf.shape[1]

    def swap_store(k):
        if swap_stores is None or swap_stores[k] is None:
            return []
        first, number = swap_stores[k]
        return store(result_ref, [(refs[0].at[pl.ds(0, number)], True, first)], sems, 1)

    @pl.when(jnp.logical_not(at_end()))
    def _():
        copies = swap_store(0)
        for copy in copies:
            copy.start()
        products(blocks, weights, tokens, (own_buf, swap_ref))
        copies += store(result_ref, [(own_buf, False, start)], sems)
        copies[-1].start()
        for copy in copies:
            copy.wait()

    @pl.when(at_end())
    def _():
        copies = swap_store(1)
        if back_start is not None:
            back_ref = refs[1]
            number = back_ref.shape[0]
            copies += store(result_ref, [(back_ref.at[:, pl.ds(0, rows)], False, back_start)], sems)
            copies.append(
                pltpu.make_async_copy(back_ref.at[:, pl.ds(rows, rows)], swap_ref.at[pl.ds(0, number)], sems.at[2])
            )
        copy_all(copies)


def own_hidden(tokens, weights, blocks, start, size, result, swapped=None, back=None):
    rows = tokens[0].shape[1]
    whole = pl.BlockSpec(memory_space=pltpu.VMEM)
    in_hbm = pl.BlockSpec(memory_space=pltpu.HBM)
    operands = [*tokens, *weights]
    swap_rows = size
    if swapped is not None:
        operands.append(swapped[0])
    if back is not None:
        operands.append(back[0])
        swap_rows = max(size, back[0].shape[0])
    in_specs = [whole] * len(operands)
    aliases = {}
    if not isinstance(result, jax.ShapeDtypeStruct):
        aliases = {len(operands): 0}
        operands.append(result)
        in_specs.append(in_hbm)
    plan = (start, blocks, swapped and swapped[1], back and back[1], len(weights))
    return pl.pallas_call(
        functools.partial(own_kernel, plan),
        in_specs=in_specs,
        out_specs=[in_hbm, whole],
        out_shape=[
            jax.ShapeDtypeStruct(result.shape, result.dtype),
            jax.ShapeDtypeStruct((swap_rows, rows), result.dtype),
        ],
        scratch_shapes=[pltpu.VMEM((size, rows), result.dtype), pltpu.SemaphoreType.DMA((3,))],
        input_output_aliases=aliases,
        compiler_params=pltpu.CompilerParams(vmem_limit_bytes=VMEM),
        cost_estimate=pl.CostEstimate(flops=0, bytes_accessed=2 * size * rows, transcendentals=0),
        name="own_hidden",
    )(*operands)


def put_kernel(stores, *refs):
    result_ref, sems = refs[-2:]
    for end in (0, 1):

        @pl.when(at_end() == (end == 1))
        def _():
            parts = [
                (refs[k].at[pl.ds(0, count)], others, first) for k, others, first, count in stores[end]
            ]
            copy_all(store(result_ref, parts, sems))


def put(result, arrays, stores):
    in_hbm = pl.BlockSpec(memory_space=pltpu.HBM)
    return pl.pallas_call(
        functools.partial(put_kernel, stores),
        in_specs=[pl.BlockSpec(memory_space=pltpu.VMEM)] * len(arrays) + [in_hbm],
        out_specs=in_hbm,
        out_shape=jax.ShapeDtypeStruct(result.shape, result.dtype),
        scratch_shapes=[pltpu.SemaphoreType.DMA((len(arrays),))],
        input_output_aliases={len(arrays): 0},
        compiler_params=pltpu.CompilerParams(vmem_limit_bytes=SMALL),
        cost_estimate=pl.CostEstimate(flops=0, bytes_accessed=4 * arrays[0].size, transcendentals=0),
        name="put",
    )(*arrays, result)


def after(x, *earlier):
    return lax.optimization_barrier((x, *earlier))[0]


def folded(tokens, gate_weight, up_weight):
    rows_own = tokens.shape[0]
    columns_dev = gate_weight.shape[1]

    def between(pairs, cross=0):
        return [(s * CORES + c, t * CORES + (c ^ cross)) for s, t in pairs for c in range(CORES)]

    inward = between([(0, 1), (3, 2)])
    outward = between([(1, 0), (2, 3)])
    outward_cross = between([(1, 0), (2, 3)], 1)
    across = between([(1, 2), (2, 1)])
    other_core = [(i, i ^ 1) for i in range(LINE * CORES)]

    def send(x, pairs, name):
        with jax.named_scope(name):
            return lax.ppermute(x, "wide", pairs)

    tiles = half_of(columns_dev) // TILE
    counts = [tiles * p // 116 for p in SHARES]
    counts.append(tiles - sum(counts))
    n = [TILE * t for t in counts]
    chunks = [(sum(n[:i]), n[i]) for i in range(3)]

    mine = gate_weight.T, up_weight.T
    got = send(cut(*mine, 0, sum(n), LARGE), other_core, "swap")
    pack_01, pack_0 = pack(*mine, got, 0, chunks, ((0, 1), (0,)))
    pack_1, pack_2 = pack(*mine, got, 0, chunks, ((1,), (2,)))

    own_01 = send(pack_01, across, "own_01")
    outer_0 = send(pack_0, inward, "outer_0")
    outer_1 = send(after(pack_1, outer_0), inward, "outer_1")
    outer_2 = send(after(pack_2, outer_0), inward, "outer_2")
    far_0 = send(outer_0, across, "far_0")

    here = after(tokens, pack_0)
    blocks = [here] + [lax.ppermute(here, "narrow", [(i, i ^ d) for i in range(LINE)]) for d in (1, 2, 3)]
    x_own, x_give = arrange(blocks)
    x_outer = send(x_give, inward, "x_outer")
    x = x_own, send(x_own, other_core, "x_other"), x_outer, send(x_outer, other_core, "x_outer_other")

    far_1 = send(after(outer_1, own_01), across, "far_1")
    own_2 = send(after(pack_2, far_0), across, "own_2")

    def plan(size, sources):
        step = size if size <= 384 else size // (2 * TILE) * TILE
        cuts = [0, step, size] if step < size else [0, size]
        return [(j, k - j, [(w, g + j, u + j) for w, g, u in sources]) for j, k in zip(cuts[:-1], cuts[1:])]

    def blocks_of(i, rows):
        return plan(n[i], [(k, row, row + n[i]) for k, row in enumerate(rows)])

    second = [2 * n[0]] * 2 + [0] * 2
    far_2 = send(after(outer_2, far_1), across, "far_2")
    weights = [
        [pack_01, own_01, outer_0, far_0],
        [pack_01, own_01, outer_1, far_1],
        [pack_2, own_2, outer_2, far_2],
    ]
    blocks = [blocks_of(0, [0] * 4), blocks_of(1, second), blocks_of(2, [0] * 4)]

    (out,) = outer_hidden(x[2:], weights[0], blocks[0], n[0], True)
    back_0 = send(out, outward, "back_0")
    same, cross = outer_hidden((x[2], x[3]), weights[1], blocks[1], n[1], False)
    back_1 = send(same, outward, "back_1_same"), send(cross, outward_cross, "back_1_cross")
    outs_1 = same
    same, cross = outer_hidden((after(x[2], outs_1), x[3]), weights[2], blocks[2], n[2], False)
    back_2 = send(same, outward, "back_2_same"), send(cross, outward_cross, "back_2_cross")
    own = [(after(x[0], out), x[1]), (after(x[0], outs_1), x[1]), (after(x[0], same), x[1])]

    result = jax.ShapeDtypeStruct((columns_dev, rows_own), jnp.bfloat16)
    result, swap = own_hidden(own[0], weights[0], blocks[0], *chunks[0], result)
    swapped_0 = send(swap, other_core, "swapped_0")
    result, swap = own_hidden(
        own[1], weights[1], blocks[1], *chunks[1], result, swapped=(swapped_0, (chunks[0], None)), back=(back_0, 0)
    )
    swapped_1 = send(swap, other_core, "swapped_1")
    result, swap = own_hidden(
        own[2], weights[2], blocks[2], *chunks[2], result, swapped=(swapped_1, (chunks[1], chunks[0]))
    )
    swapped_2 = send(after(swap, back_2[0], *back_1), other_core, "swapped_2")
    result = put(result, back_1, ([], [(0, False, *chunks[1]), (1, True, *chunks[1])]))
    stores = [(0, True, *chunks[2])], [(1, False, *chunks[2]), (2, True, *chunks[2])]
    return put(result, (swapped_2, *back_2), stores).T


def solution(mesh):
    in_specs = (P("wide", "narrow"), P("wide", "narrow"), P("wide", "narrow"))
    out_specs = P("wide", "narrow")
    local = folded if mesh.shape["wide"] == LINE * CORES else gathered_everywhere
    return jax.shard_map(local, mesh=mesh, in_specs=in_specs, out_specs=out_specs, check_vma=False)
```

time: 119 us -> 115 us (0.966)
  waiting for transfers between devices: 79.3 us -> 68.8 us
  starting transfers between devices: 33.4 us -> 39.2 us
    ppermute x19 -> x20, waiting for transfers between devices: 70.4 us -> 63.6 us  [send(): return lax.ppermute(x, 'wide', pairs)]
    ppermute x19 -> x20, starting transfers between devices: 29.9 us -> 35.6 us  [send(): return lax.ppermute(x, 'wide', pairs)]
    ppermute x3, waiting for transfers between devices: 8.85 us -> 5.23 us  [folded(): lax.ppermute(here, 'narrow', [(i, i ^ d) for i in range(LINE)])]
    pallas_call x8 -> x10, Pallas kernels: 4.19 us -> 5.05 us  [the longest x1 2.39 us: cut(): pl.pallas_call(functools.partial(cut_kernel, start, size), in_specs=[in_h...]
  transfers between devices with their start and end apart: 22 -> 23, of which waited for: 12 -> 13; matrix products, arithmetic and copies ran while one was open for 0% -> 0% of each run, Pallas kernels for 2% -> 3%
where the time goes in v2:
time: 115 us
  waiting for transfers between devices  68.8 us (60%)
  starting transfers between devices  39.2 us (34%)
  Pallas kernels  6.71 us (6%)
    ppermute x20, waiting for transfers between devices, send(): return lax.ppermute(x, 'wide', pairs)  63.6 us
    ppermute x20, starting transfers between devices, send(): return lax.ppermute(x, 'wide', pairs)  35.6 us
    ppermute x3, waiting for transfers between devices, folded(): lax.ppermute(here, 'narrow', [(i, i ^ d) for i in range(LINE)])  5.23 us
    ppermute x3, starting transfers between devices, folded(): lax.ppermute(here, 'narrow', [(i, i ^ d) for i in range(LINE)])  3.55 us
    pallas_call x1, Pallas kernels, cut(): pl.pallas_call(functools.partial(cut_kernel, start, size), in_specs=[in_h...  2.39 us
  transfers between devices with their start and end apart: 23, of which 13 were waited for; matrix products, arithmetic and copies ran while one was open for 0% of the time, Pallas kernels for 3%

profile of v2, /device:TPU:0, one launch (start us, length us, event | category | flops | bytes accessed | tf_op | source)
XLA Modules:
  0.0 115.0 jit_solution(12905793073719375899)
XLA Ops:
  0.0 0.0 copy-start.1
  0.0 0.0 copy-start
  0.0 2.4 %cut.1 = bf16[3712,128]{1,0:T(8,128)(2,1)} custom-call(bf16[3696,128]{1,0:T(8,128)(2,1)} %bitcast.3, bf16[3696,128]{1,0:T(8,128)(2,1)} %bitcast.6), custom_call_target="tpu_custom_call" | custom-call | bytes 1892352 | tf_op jit(solution)/shard_map/cut/pallas_call | solution.py:76
  2.4 0.0 copy-start.2
  2.4 0.5 collective-permute-start
  2.9 2.4 %collective-permute-done.got_ref = bf16[3712,128]{1,0:T(8,128)(2,1)S(1)} collective-permute-done((bf16[3712,128]{1,0:T(8,128)(2,1)}, bf16[3712,128]{1,0:T(8,128)(2,1)S(1)}, u32[]{:S(2)}, u32[]{:S(2)}) %collective-permute-start) | collective-permute-done | bytes 950304 | tf_op jit(solution)/shard_map/swap/ppermute | solution.py:326
  5.3 0.0 copy-done.1
  5.3 0.0 copy-done
  5.3 0.5 pack.2
  5.8 4.9 %collective-permute-start.7 = (bf16[1408,256]{1,0:T(8,128)(2,1)S(1)}, bf16[1408,256]{1,0:T(8,128)(2,1)S(1)}, u32[]{:S(2)}, u32[]{:S(2)}) collective-permute-start(bf16[1408,256]{1,0:T(8,128)(2,1)S(1)} %get-tuple-element.32), channel_id=1, source_target_pairs={{0,8},{4,12},{24,16},{28,20},{1,9},{5,13},{25,17},{29,21},{2,10},{... | collective-permute-start | bytes 2162696 | tf_op jit(solution)/shard_map/outer_0/ppermute | solution.py:326
  10.7 0.8 collective-permute-start.6
  11.5 0.0 copy-done.2
  11.5 2.5 %collective-permute-start.3 = (bf16[256,256]{1,0:T(8,128)(2,1)S(1)}, bf16[256,256]{1,0:T(8,128)(2,1)S(1)}, u32[]{:S(2)}, u32[]{:S(2)}) collective-permute-start(bf16[256,256]{1,0:T(8,128)(2,1)S(1)} %copy-done.2), channel_id=1, source_target_pairs={{0,3},{1,2},{2,1},{3,0},{4,7},{5,6},{6,5},{7,4},{8,11},{9,10},{10,... | collective-permute-start | bytes 393224 | tf_op jit(solution)/shard_map/ppermute | solution.py:346
  14.0 0.5 collective-permute-start.2
  14.5 0.5 collective-permute-start.1
  15.0 0.3 pack.3
  15.3 2.7 %collective-permute-done.3.refs_3_ = bf16[256,256]{1,0:T(8,128)(2,1)S(1)} collective-permute-done((bf16[256,256]{1,0:T(8,128)(2,1)S(1)}, bf16[256,256]{1,0:T(8,128)(2,1)S(1)}, u32[]{:S(2)}, u32[]{:S(2)}) %collective-permute-start.3) | collective-permute-done | bytes 131104 | tf_op jit(solution)/shard_map/ppermute | solution.py:346
  18.0 2.5 %collective-permute-done.2.refs_2_ = bf16[256,256]{1,0:T(8,128)(2,1)S(1)} collective-permute-done((bf16[256,256]{1,0:T(8,128)(2,1)S(1)}, bf16[256,256]{1,0:T(8,128)(2,1)S(1)}, u32[]{:S(2)}, u32[]{:S(2)}) %collective-permute-start.2) | collective-permute-done | bytes 131104 | tf_op jit(solution)/shard_map/ppermute | solution.py:346
  20.5 0.1 collective-permute-done.1.refs_1_
  20.6 0.2 arrange.1
  20.8 4.0 %collective-permute-start.4 = (bf16[1024,256]{1,0:T(8,128)(2,1)S(1)}, bf16[1024,256]{1,0:T(8,128)(2,1)S(1)}, u32[]{:S(2)}, u32[]{:S(2)}) collective-permute-start(bf16[1024,256]{1,0:T(8,128)(2,1)S(1)} %get-tuple-element.35), channel_id=1, source_target_pairs={{0,8},{4,12},{24,16},{28,20},{1,9},{5,13},{25,17},{29,21},{2,10},{... | collective-permute-start | bytes 1572872 | tf_op jit(solution)/shard_map/x_outer/ppermute | solution.py:326
  24.8 2.4 %collective-permute-done.7.refs_4_ = bf16[1408,256]{1,0:T(8,128)(2,1)S(1)} collective-permute-done((bf16[1408,256]{1,0:T(8,128)(2,1)S(1)}, bf16[1408,256]{1,0:T(8,128)(2,1)S(1)}, u32[]{:S(2)}, u32[]{:S(2)}) %collective-permute-start.7) | collective-permute-done | bytes 720928 | tf_op jit(solution)/shard_map/outer_0/ppermute | solution.py:326
  27.2 4.4 %collective-permute-start.8 = (bf16[1472,256]{1,0:T(8,128)(2,1)S(1)}, bf16[1472,256]{1,0:T(8,128)(2,1)S(1)}, u32[]{:S(2)}, u32[]{:S(2)}) collective-permute-start(bf16[1472,256]{1,0:T(8,128)(2,1)S(1)} %get-tuple-element.38), channel_id=1, source_target_pairs={{0,8},{4,12},{24,16},{28,20},{1,9},{5,13},{25,17},{29,21},{2,10},{... | collective-permute-start | bytes 2261000 | tf_op jit(solution)/shard_map/outer_1/ppermute | solution.py:326
  31.6 0.7 collective-permute-start.10
  32.3 6.1 %collective-permute-done.4.refs_0_ = bf16[1024,256]{1,0:T(8,128)(2,1)S(1)} collective-permute-done((bf16[1024,256]{1,0:T(8,128)(2,1)S(1)}, bf16[1024,256]{1,0:T(8,128)(2,1)S(1)}, u32[]{:S(2)}, u32[]{:S(2)}) %collective-permute-start.4) | collective-permute-done | bytes 524320 | tf_op jit(solution)/shard_map/x_outer/ppermute | solution.py:326
  38.4 0.0 collective-permute-start.5
  38.4 15.3 %collective-permute-done.8.refs_4_ = bf16[1472,256]{1,0:T(8,128)(2,1)S(1)} collective-permute-done((bf16[1472,256]{1,0:T(8,128)(2,1)S(1)}, bf16[1472,256]{1,0:T(8,128)(2,1)S(1)}, u32[]{:S(2)}, u32[]{:S(2)}) %collective-permute-start.8) | collective-permute-done | bytes 753696 | tf_op jit(solution)/shard_map/outer_1/ppermute | solution.py:326
  53.7 0.0 collective-permute-done.6.refs_3_
  53.7 0.7 collective-permute-start.9
  54.4 0.1 collective-permute-start.14
  54.5 0.0 collective-permute-done.5.refs_1_
  54.5 0.0 collective-permute-done.10.refs_5_
  54.6 1.3 %collective-permute-start.16 = (bf16[704,512]{1,0:T(8,128)(2,1)S(1)}, bf16[704,512]{1,0:T(8,128)(2,1)S(1)}, u32[]{:S(2)}, u32[]{:S(2)}) collective-permute-start(bf16[704,512]{1,0:T(8,128)(2,1)S(1)} %outer_hidden.5), channel_id=1, source_target_pairs={{8,0},{12,4},{16,24},{20,28},{9,1},{13,5},{17,25},{21,29},{10,2},{... | collective-permute-start | bytes 2162696 | tf_op jit(solution)/shard_map/back_0/ppermute | solution.py:326
  55.9 11.6 %collective-permute-start.12 = (bf16[832,256]{1,0:T(8,128)(2,1)S(1)}, bf16[832,256]{1,0:T(8,128)(2,1)S(1)}, u32[]{:S(2)}, u32[]{:S(2)}) collective-permute-start(bf16[832,256]{1,0:T(8,128)(2,1)S(1)} %get-tuple-element.44.refs_2_), channel_id=1, source_target_pairs={{0,8},{4,12},{24,16},{28,20},{1,9},{5,13},{25,17},{29,21},{2,10},{... | collective-permute-start | bytes 1277960 | tf_op jit(solution)/shard_map/outer_2/ppermute | solution.py:326
  67.5 0.0 collective-permute-done.14.refs_1_
  67.5 0.1 own_hidden.3
  67.5 0.1 collective-permute-start.15
  67.6 0.7 collective-permute-start.11
  68.3 6.9 %collective-permute-done.12.refs_4_ = bf16[832,256]{1,0:T(8,128)(2,1)S(1)} collective-permute-done((bf16[832,256]{1,0:T(8,128)(2,1)S(1)}, bf16[832,256]{1,0:T(8,128)(2,1)S(1)}, u32[]{:S(2)}, u32[]{:S(2)}) %collective-permute-start.12) | collective-permute-done | bytes 426016 | tf_op jit(solution)/shard_map/outer_2/ppermute | solution.py:326
  75.2 0.0 collective-permute-done.9.refs_5_
  75.2 0.7 collective-permute-start.13
  75.9 0.0 collective-permute-done.15.refs_6_
  75.9 4.4 %collective-permute-done.16.refs_7_ = bf16[704,512]{1,0:T(8,128)(2,1)S(1)} collective-permute-done((bf16[704,512]{1,0:T(8,128)(2,1)S(1)}, bf16[704,512]{1,0:T(8,128)(2,1)S(1)}, u32[]{:S(2)}, u32[]{:S(2)}) %collective-permute-start.16) | collective-permute-done | bytes 720928 | tf_op jit(solution)/shard_map/back_0/ppermute | solution.py:326
  80.3 0.8 own_hidden.4
  81.1 0.1 collective-permute-start.17
  81.1 1.3 %collective-permute-start.20 = (bf16[736,256]{1,0:T(8,128)(2,1)S(1)}, bf16[736,256]{1,0:T(8,128)(2,1)S(1)}, u32[]{:S(2)}, u32[]{:S(2)}) collective-permute-start(bf16[736,256]{1,0:T(8,128)(2,1)S(1)} %get-tuple-element.55), channel_id=1, source_target_pairs={{8,4},{12,0},{16,28},{20,24},{9,5},{13,1},{17,29},{21,25},{10,6},{... | collective-permute-start | bytes 1130504 | tf_op jit(solution)/shard_map/back_1_cross/ppermute | solution.py:326
  82.4 1.3 %collective-permute-start.19 = (bf16[736,256]{1,0:T(8,128)(2,1)S(1)}, bf16[736,256]{1,0:T(8,128)(2,1)S(1)}, u32[]{:S(2)}, u32[]{:S(2)}) collective-permute-start(bf16[736,256]{1,0:T(8,128)(2,1)S(1)} %get-tuple-element.40), channel_id=1, source_target_pairs={{8,0},{12,4},{16,24},{20,28},{9,1},{13,5},{17,25},{21,29},{10,2},{... | collective-permute-start | bytes 1130504 | tf_op jit(solution)/shard_map/back_1_same/ppermute | solution.py:326
  83.7 0.0 collective-permute-done.11.refs_3_
  83.7 0.0 collective-permute-done.13.refs_5_
  83.8 1.3 %collective-permute-start.18 = (bf16[416,256]{1,0:T(8,128)(2,1)S(1)}, bf16[416,256]{1,0:T(8,128)(2,1)S(1)}, u32[]{:S(2)}, u32[]{:S(2)}) collective-permute-start(bf16[416,256]{1,0:T(8,128)(2,1)S(1)} %get-tuple-element.46), channel_id=1, source_target_pairs={{8,0},{12,4},{16,24},{20,28},{9,1},{13,5},{17,25},{21,29},{10,2},{... | collective-permute-start | bytes 638984 | tf_op jit(solution)/shard_map/back_2_same/ppermute | solution.py:326
  85.1 1.3 %collective-permute-start.22 = (bf16[416,256]{1,0:T(8,128)(2,1)S(1)}, bf16[416,256]{1,0:T(8,128)(2,1)S(1)}, u32[]{:S(2)}, u32[]{:S(2)}) collective-permute-start(bf16[416,256]{1,0:T(8,128)(2,1)S(1)} %get-tuple-element.57), channel_id=1, source_target_pairs={{8,4},{12,0},{16,28},{20,24},{9,5},{13,1},{17,29},{21,25},{10,6},{... | collective-permute-start | bytes 638984 | tf_op jit(solution)/shard_map/back_2_cross/ppermute | solution.py:326
  86.4 0.0 collective-permute-done.17.refs_6_
  86.4 0.8 own_hidden.5
  87.2 9.8 %collective-permute-done.20.refs_1_ = bf16[736,256]{1,0:T(8,128)(2,1)S(1)} collective-permute-done((bf16[736,256]{1,0:T(8,128)(2,1)S(1)}, bf16[736,256]{1,0:T(8,128)(2,1)S(1)}, u32[]{:S(2)}, u32[]{:S(2)}) %collective-permute-start.20) | collective-permute-done | bytes 376864 | tf_op jit(solution)/shard_map/back_1_cross/ppermute | solution.py:326
  97.0 8.5 %collective-permute-done.19.refs_0_ = bf16[736,256]{1,0:T(8,128)(2,1)S(1)} collective-permute-done((bf16[736,256]{1,0:T(8,128)(2,1)S(1)}, bf16[736,256]{1,0:T(8,128)(2,1)S(1)}, u32[]{:S(2)}, u32[]{:S(2)}) %collective-permute-start.19) | collective-permute-done | bytes 376864 | tf_op jit(solution)/shard_map/back_1_same/ppermute | solution.py:326
  105.5 4.6 %collective-permute-done.18.refs_1_ = bf16[416,256]{1,0:T(8,128)(2,1)S(1)} collective-permute-done((bf16[416,256]{1,0:T(8,128)(2,1)S(1)}, bf16[416,256]{1,0:T(8,128)(2,1)S(1)}, u32[]{:S(2)}, u32[]{:S(2)}) %collective-permute-start.18) | collective-permute-done | bytes 213024 | tf_op jit(solution)/shard_map/back_2_same/ppermute | solution.py:326
  110.1 0.0 collective-permute-start.21
  110.1 0.9 put.2.refs_3_
  111.0 3.3 %collective-permute-done.22.refs_2_ = bf16[416,256]{1,0:T(8,128)(2,1)S(1)} collective-permute-done((bf16[416,256]{1,0:T(8,128)(2,1)S(1)}, bf16[416,256]{1,0:T(8,128)(2,1)S(1)}, u32[]{:S(2)}, u32[]{:S(2)}) %collective-permute-start.22) | collective-permute-done | bytes 213024 | tf_op jit(solution)/shard_map/back_2_cross/ppermute | solution.py:326
  114.2 0.0 collective-permute-done.21.refs_0_
  114.2 0.8 put.3
  (3 shorter events, 0.1 us)
Async XLA Ops:
  0.0 5.3 %copy-start.1 = (bf16[128,3696]{0,1:T(8,128)(2,1)S(1)}, bf16[128,3696]{0,1:T(8,128)(2,1)}, u32[]{:S(2)}) copy-start(bf16[128,3696]{0,1:T(8,128)(2,1)} %param.5) | copy-start | bytes 2838532
  0.0 5.3 %copy-start = (bf16[128,3696]{0,1:T(8,128)(2,1)S(1)}, bf16[128,3696]{0,1:T(8,128)(2,1)}, u32[]{:S(2)}) copy-start(bf16[128,3696]{0,1:T(8,128)(2,1)} %param.4) | copy-start | bytes 2838532
  2.4 9.1 %copy-start.2 = (bf16[256,256]{1,0:T(8,128)(2,1)S(1)}, bf16[256,256]{1,0:T(8,128)(2,1)}, u32[]{:S(2)}) copy-start(bf16[256,256]{1,0:T(8,128)(2,1)} %refs_0_) | copy-start | bytes 393220
  2.4 2.9 %collective-permute-start = (bf16[3712,128]{1,0:T(8,128)(2,1)}, bf16[3712,128]{1,0:T(8,128)(2,1)S(1)}, u32[]{:S(2)}, u32[]{:S(2)}) collective-permute-start(bf16[3712,128]{1,0:T(8,128)(2,1)} %cut.1), channel_id=1, source_target_pairs={{0,4},{4,0},{8,12},{12,8},{16,20},{20,16},{24,28},{28,24},{1,5},{5... | collective-permute-start | bytes 2850824 | tf_op jit(solution)/shard_map/swap/ppermute | solution.py:326
  5.8 21.3 %collective-permute-start.7 = (bf16[1408,256]{1,0:T(8,128)(2,1)S(1)}, bf16[1408,256]{1,0:T(8,128)(2,1)S(1)}, u32[]{:S(2)}, u32[]{:S(2)}) collective-permute-start(bf16[1408,256]{1,0:T(8,128)(2,1)S(1)} %get-tuple-element.32), channel_id=1, source_target_pairs={{0,8},{4,12},{24,16},{28,20},{1,9},{5,13},{25,17},{29,21},{2,10},{... | collective-permute-start | bytes 2162696 | tf_op jit(solution)/shard_map/outer_0/ppermute | solution.py:326
  10.7 43.0 %collective-permute-start.6 = (bf16[2880,256]{1,0:T(8,128)(2,1)S(1)}, bf16[2880,256]{1,0:T(8,128)(2,1)S(1)}, u32[]{:S(2)}, u32[]{:S(2)}) collective-permute-start(bf16[2880,256]{1,0:T(8,128)(2,1)S(1)} %get-tuple-element.36.refs_2_), channel_id=1, source_target_pairs={{8,16},{12,20},{16,8},{20,12},{9,17},{13,21},{17,9},{21,13},{10,18... | collective-permute-start | bytes 4423688 | tf_op jit(solution)/shard_map/own_01/ppermute | solution.py:326
  11.5 6.5 %collective-permute-start.3 = (bf16[256,256]{1,0:T(8,128)(2,1)S(1)}, bf16[256,256]{1,0:T(8,128)(2,1)S(1)}, u32[]{:S(2)}, u32[]{:S(2)}) collective-permute-start(bf16[256,256]{1,0:T(8,128)(2,1)S(1)} %copy-done.2), channel_id=1, source_target_pairs={{0,3},{1,2},{2,1},{3,0},{4,7},{5,6},{6,5},{7,4},{8,11},{9,10},{10,... | collective-permute-start | bytes 393224 | tf_op jit(solution)/shard_map/ppermute | solution.py:346
  14.0 6.5 %collective-permute-start.2 = (bf16[256,256]{1,0:T(8,128)(2,1)S(1)}, bf16[256,256]{1,0:T(8,128)(2,1)S(1)}, u32[]{:S(2)}, u32[]{:S(2)}) collective-permute-start(bf16[256,256]{1,0:T(8,128)(2,1)S(1)} %copy-done.2), channel_id=1, source_target_pairs={{0,2},{1,3},{2,0},{3,1},{4,6},{5,7},{6,4},{7,5},{8,10},{9,11},{10,... | collective-permute-start | bytes 393224 | tf_op jit(solution)/shard_map/ppermute | solution.py:346
  14.5 6.1 %collective-permute-start.1 = (bf16[256,256]{1,0:T(8,128)(2,1)S(1)}, bf16[256,256]{1,0:T(8,128)(2,1)S(1)}, u32[]{:S(2)}, u32[]{:S(2)}) collective-permute-start(bf16[256,256]{1,0:T(8,128)(2,1)S(1)} %copy-done.2), channel_id=1, source_target_pairs={{0,1},{1,0},{2,3},{3,2},{4,5},{5,4},{6,7},{7,6},{8,9},{9,8},{10,11... | collective-permute-start | bytes 393224 | tf_op jit(solution)/shard_map/ppermute | solution.py:346
  20.8 17.6 %collective-permute-start.4 = (bf16[1024,256]{1,0:T(8,128)(2,1)S(1)}, bf16[1024,256]{1,0:T(8,128)(2,1)S(1)}, u32[]{:S(2)}, u32[]{:S(2)}) collective-permute-start(bf16[1024,256]{1,0:T(8,128)(2,1)S(1)} %get-tuple-element.35), channel_id=1, source_target_pairs={{0,8},{4,12},{24,16},{28,20},{1,9},{5,13},{25,17},{29,21},{2,10},{... | collective-permute-start | bytes 1572872 | tf_op jit(solution)/shard_map/x_outer/ppermute | solution.py:326
  27.2 26.6 %collective-permute-start.8 = (bf16[1472,256]{1,0:T(8,128)(2,1)S(1)}, bf16[1472,256]{1,0:T(8,128)(2,1)S(1)}, u32[]{:S(2)}, u32[]{:S(2)}) collective-permute-start(bf16[1472,256]{1,0:T(8,128)(2,1)S(1)} %get-tuple-element.38), channel_id=1, source_target_pairs={{0,8},{4,12},{24,16},{28,20},{1,9},{5,13},{25,17},{29,21},{2,10},{... | collective-permute-start | bytes 2261000 | tf_op jit(solution)/shard_map/outer_1/ppermute | solution.py:326
  31.6 23.0 %collective-permute-start.10 = (bf16[1408,256]{1,0:T(8,128)(2,1)S(1)}, bf16[1408,256]{1,0:T(8,128)(2,1)S(1)}, u32[]{:S(2)}, u32[]{:S(2)}) collective-permute-start(bf16[1408,256]{1,0:T(8,128)(2,1)S(1)} %collective-permute-done.7.refs_4_), channel_id=1, source_target_pairs={{8,16},{12,20},{16,8},{20,12},{9,17},{13,21},{17,9},{21,13},{10,18... | collective-permute-start | bytes 2162696 | tf_op jit(solution)/shard_map/far_0/ppermute | solution.py:326
  38.4 16.1 %collective-permute-start.5 = (bf16[1024,256]{1,0:T(8,128)(2,1)S(1)}, bf16[1024,256]{1,0:T(8,128)(2,1)S(1)}, u32[]{:S(2)}, u32[]{:S(2)}) collective-permute-start(bf16[1024,256]{1,0:T(8,128)(2,1)S(1)} %collective-permute-done.4.refs_0_), channel_id=1, source_target_pairs={{0,4},{4,0},{8,12},{12,8},{16,20},{20,16},{24,28},{28,24},{1,5},{5... | collective-permute-start | bytes 1572872 | tf_op jit(solution)/shard_map/x_outer_other/ppermute | solution.py:326
  53.7 21.4 %collective-permute-start.9 = (bf16[1472,256]{1,0:T(8,128)(2,1)S(1)}, bf16[1472,256]{1,0:T(8,128)(2,1)S(1)}, u32[]{:S(2)}, u32[]{:S(2)}) collective-permute-start(bf16[1472,256]{1,0:T(8,128)(2,1)S(1)} %collective-permute-done.8.refs_4_), channel_id=1, source_target_pairs={{8,16},{12,20},{16,8},{20,12},{9,17},{13,21},{17,9},{21,13},{10,18... | collective-permute-start | bytes 2261000 | tf_op jit(solution)/shard_map/far_1/ppermute | solution.py:326
  54.4 13.0 %collective-permute-start.14 = (bf16[1024,256]{1,0:T(8,128)(2,1)S(1)}, bf16[1024,256]{1,0:T(8,128)(2,1)S(1)}, u32[]{:S(2)}, u32[]{:S(2)}) collective-permute-start(bf16[1024,256]{1,0:T(8,128)(2,1)S(1)} %get-tuple-element.49.refs_0_), channel_id=1, source_target_pairs={{0,4},{4,0},{8,12},{12,8},{16,20},{20,16},{24,28},{28,24},{1,5},{5... | collective-permute-start | bytes 1572872 | tf_op jit(solution)/shard_map/x_other/ppermute | solution.py:326
  54.6 25.7 %collective-permute-start.16 = (bf16[704,512]{1,0:T(8,128)(2,1)S(1)}, bf16[704,512]{1,0:T(8,128)(2,1)S(1)}, u32[]{:S(2)}, u32[]{:S(2)}) collective-permute-start(bf16[704,512]{1,0:T(8,128)(2,1)S(1)} %outer_hidden.5), channel_id=1, source_target_pairs={{8,0},{12,4},{16,24},{20,28},{9,1},{13,5},{17,25},{21,29},{10,2},{... | collective-permute-start | bytes 2162696 | tf_op jit(solution)/shard_map/back_0/ppermute | solution.py:326
  55.9 19.3 %collective-permute-start.12 = (bf16[832,256]{1,0:T(8,128)(2,1)S(1)}, bf16[832,256]{1,0:T(8,128)(2,1)S(1)}, u32[]{:S(2)}, u32[]{:S(2)}) collective-permute-start(bf16[832,256]{1,0:T(8,128)(2,1)S(1)} %get-tuple-element.44.refs_2_), channel_id=1, source_target_pairs={{0,8},{4,12},{24,16},{28,20},{1,9},{5,13},{25,17},{29,21},{2,10},{... | collective-permute-start | bytes 1277960 | tf_op jit(solution)/shard_map/outer_2/ppermute | solution.py:326
  67.5 8.4 %collective-permute-start.15 = (bf16[704,256]{1,0:T(8,128)(2,1)S(1)}, bf16[704,256]{1,0:T(8,128)(2,1)S(1)}, u32[]{:S(2)}, u32[]{:S(2)}) collective-permute-start(bf16[704,256]{1,0:T(8,128)(2,1)S(1)} %get-tuple-element.50), channel_id=1, source_target_pairs={{0,4},{4,0},{8,12},{12,8},{16,20},{20,16},{24,28},{28,24},{1,5},{5... | collective-permute-start | bytes 1081352 | tf_op jit(solution)/shard_map/swapped_0/ppermute | solution.py:326
  67.6 16.1 %collective-permute-start.11 = (bf16[832,256]{1,0:T(8,128)(2,1)S(1)}, bf16[832,256]{1,0:T(8,128)(2,1)S(1)}, u32[]{:S(2)}, u32[]{:S(2)}) collective-permute-start(bf16[832,256]{1,0:T(8,128)(2,1)S(1)} %get-tuple-element.44.refs_2_), channel_id=1, source_target_pairs={{8,16},{12,20},{16,8},{20,12},{9,17},{13,21},{17,9},{21,13},{10,18... | collective-permute-start | bytes 1277960 | tf_op jit(solution)/shard_map/own_2/ppermute | solution.py:326
  75.2 8.6 %collective-permute-start.13 = (bf16[832,256]{1,0:T(8,128)(2,1)S(1)}, bf16[832,256]{1,0:T(8,128)(2,1)S(1)}, u32[]{:S(2)}, u32[]{:S(2)}) collective-permute-start(bf16[832,256]{1,0:T(8,128)(2,1)S(1)} %collective-permute-done.12.refs_4_), channel_id=1, source_target_pairs={{8,16},{12,20},{16,8},{20,12},{9,17},{13,21},{17,9},{21,13},{10,18... | collective-permute-start | bytes 1277960 | tf_op jit(solution)/shard_map/far_2/ppermute | solution.py:326
  81.1 5.3 %collective-permute-start.17 = (bf16[736,256]{1,0:T(8,128)(2,1)S(1)}, bf16[736,256]{1,0:T(8,128)(2,1)S(1)}, u32[]{:S(2)}, u32[]{:S(2)}) collective-permute-start(bf16[736,256]{1,0:T(8,128)(2,1)S(1)} %get-tuple-element.52), channel_id=1, source_target_pairs={{0,4},{4,0},{8,12},{12,8},{16,20},{20,16},{24,28},{28,24},{1,5},{5... | collective-permute-start | bytes 1130504 | tf_op jit(solution)/shard_map/swapped_1/ppermute | solution.py:326
  81.1 15.9 %collective-permute-start.20 = (bf16[736,256]{1,0:T(8,128)(2,1)S(1)}, bf16[736,256]{1,0:T(8,128)(2,1)S(1)}, u32[]{:S(2)}, u32[]{:S(2)}) collective-permute-start(bf16[736,256]{1,0:T(8,128)(2,1)S(1)} %get-tuple-element.55), channel_id=1, source_target_pairs={{8,4},{12,0},{16,28},{20,24},{9,5},{13,1},{17,29},{21,25},{10,6},{... | collective-permute-start | bytes 1130504 | tf_op jit(solution)/shard_map/back_1_cross/ppermute | solution.py:326
  82.4 23.1 %collective-permute-start.19 = (bf16[736,256]{1,0:T(8,128)(2,1)S(1)}, bf16[736,256]{1,0:T(8,128)(2,1)S(1)}, u32[]{:S(2)}, u32[]{:S(2)}) collective-permute-start(bf16[736,256]{1,0:T(8,128)(2,1)S(1)} %get-tuple-element.40), channel_id=1, source_target_pairs={{8,0},{12,4},{16,24},{20,28},{9,1},{13,5},{17,25},{21,29},{10,2},{... | collective-permute-start | bytes 1130504 | tf_op jit(solution)/shard_map/back_1_same/ppermute | solution.py:326
  83.8 26.3 %collective-permute-start.18 = (bf16[416,256]{1,0:T(8,128)(2,1)S(1)}, bf16[416,256]{1,0:T(8,128)(2,1)S(1)}, u32[]{:S(2)}, u32[]{:S(2)}) collective-permute-start(bf16[416,256]{1,0:T(8,128)(2,1)S(1)} %get-tuple-element.46), channel_id=1, source_target_pairs={{8,0},{12,4},{16,24},{20,28},{9,1},{13,5},{17,25},{21,29},{10,2},{... | collective-permute-start | bytes 638984 | tf_op jit(solution)/shard_map/back_2_same/ppermute | solution.py:326
  85.1 29.1 %collective-permute-start.22 = (bf16[416,256]{1,0:T(8,128)(2,1)S(1)}, bf16[416,256]{1,0:T(8,128)(2,1)S(1)}, u32[]{:S(2)}, u32[]{:S(2)}) collective-permute-start(bf16[416,256]{1,0:T(8,128)(2,1)S(1)} %get-tuple-element.57), channel_id=1, source_target_pairs={{8,4},{12,0},{16,28},{20,24},{9,5},{13,1},{17,29},{21,25},{10,6},{... | collective-permute-start | bytes 638984 | tf_op jit(solution)/shard_map/back_2_cross/ppermute | solution.py:326
  110.1 4.2 %collective-permute-start.21 = (bf16[416,256]{1,0:T(8,128)(2,1)S(1)}, bf16[416,256]{1,0:T(8,128)(2,1)S(1)}, u32[]{:S(2)}, u32[]{:S(2)}) collective-permute-start(bf16[416,256]{1,0:T(8,128)(2,1)S(1)} %get-tuple-element.56), channel_id=1, source_target_pairs={{0,4},{4,0},{8,12},{12,8},{16,20},{20,16},{24,28},{28,24},{1,5},{5... | collective-permute-start | bytes 638984 | tf_op jit(solution)/shard_map/swapped_2/ppermute | solution.py:326

commit v3 on v2

--- a/solution.py
+++ b/solution.py
@@ -10,7 +10,7 @@
 CORES = 2
 LINE = 4
 TILE = 16
-SHARES = (44, 46)
+SHARES = (44, 48)
 TURN = (0, 3, 1, 2)
 VMEM = 24 * 1024 * 1024
 SMALL = 1024 * 1024
@@ -348,7 +348,7 @@
     x_outer = send(x_give, inward, "x_outer")
     x = x_own, send(x_own, other_core, "x_other"), x_outer, send(x_outer, other_core, "x_outer_other")
 
-    far_1 = send(after(outer_1, own_01), across, "far_1")
+    far_1 = send(after(outer_1, own_01, x[3]), across, "far_1")
     own_2 = send(after(pack_2, far_0), across, "own_2")
 
     def plan(size, sources):
@@ -360,36 +360,35 @@
         return plan(n[i], [(k, row, row + n[i]) for k, row in enumerate(rows)])
 
     second = [2 * n[0]] * 2 + [0] * 2
-    far_2 = send(after(outer_2, far_1), across, "far_2")
     weights = [
         [pack_01, own_01, outer_0, far_0],
         [pack_01, own_01, outer_1, far_1],
-        [pack_2, own_2, outer_2, far_2],
     ]
     blocks = [blocks_of(0, [0] * 4), blocks_of(1, second), blocks_of(2, [0] * 4)]
 
     (out,) = outer_hidden(x[2:], weights[0], blocks[0], n[0], True)
     back_0 = send(out, outward, "back_0")
-    same, cross = outer_hidden((x[2], x[3]), weights[1], blocks[1], n[1], False)
-    back_1 = send(same, outward, "back_1_same"), send(cross, outward_cross, "back_1_cross")
-    outs_1 = same
-    same, cross = outer_hidden((after(x[2], outs_1), x[3]), weights[2], blocks[2], n[2], False)
+    result = jax.ShapeDtypeStruct((columns_dev, rows_own), jnp.bfloat16)
+    first_own = after(x[0], out), x[1]
+    result, swap = own_hidden(first_own, weights[0], blocks[0], *chunks[0], result)
+    swapped_0 = send(swap, other_core, "swapped_0")
+    (out_1,) = outer_hidden((after(x[2], swap), x[3]), weights[1], blocks[1], n[1], True)
+    back_1 = send(out_1, outward, "back_1")
+    far_2 = send(after(outer_2, out_1), across, "far_2")
+    weights.append([pack_2, own_2, outer_2, far_2])
+    same, cross = outer_hidden((after(x[2], out_1), x[3]), weights[2], blocks[2], n[2], False)
     back_2 = send(same, outward, "back_2_same"), send(cross, outward_cross, "back_2_cross")
-    own = [(after(x[0], out), x[1]), (after(x[0], outs_1), x[1]), (after(x[0], same), x[1])]
-
-    result = jax.ShapeDtypeStruct((columns_dev, rows_own), jnp.bfloat16)
-    result, swap = own_hidden(own[0], weights[0], blocks[0], *chunks[0], result)
-    swapped_0 = send(swap, other_core, "swapped_0")
+    own = [None, (after(x[0], out_1, own_2), x[1]), (after(x[0], same), x[1])]
+
     result, swap = own_hidden(
         own[1], weights[1], blocks[1], *chunks[1], result, swapped=(swapped_0, (chunks[0], None)), back=(back_0, 0)
     )
     swapped_1 = send(swap, other_core, "swapped_1")
     result, swap = own_hidden(
-        own[2], weights[2], blocks[2], *chunks[2], result, swapped=(swapped_1, (chunks[1], chunks[0]))
+        own[2], weights[2], blocks[2], *chunks[2], result, swapped=(swapped_1, (chunks[1], chunks[0])), back=(back_1, chunks[1][0])
     )
-    swapped_2 = send(after(swap, back_2[0], *back_1), other_core, "swapped_2")
-    result = put(result, back_1, ([], [(0, False, *chunks[1]), (1, True, *chunks[1])]))
-    stores = [(0, True, *chunks[2])], [(1, False, *chunks[2]), (2, True, *chunks[2])]
+    swapped_2 = send(after(swap, *back_2), other_core, "swapped_2")
+    stores = [(0, True, *chunks[2])], [(0, True, *chunks[1]), (1, False, *chunks[2]), (2, True, *chunks[2])]
     return put(result, (swapped_2, *back_2), stores).T
 
 

time: 115 us -> 110 us (0.957)
  waiting for transfers between devices: 68.8 us -> 64.9 us
    ppermute x20 -> x19, waiting for transfers between devices: 63.6 us -> 59.1 us  [send(): return lax.ppermute(x, 'wide', pairs)]
    ppermute x20 -> x19, starting transfers between devices: 35.6 us -> 35.2 us  [send(): return lax.ppermute(x, 'wide', pairs)]
  transfers between devices with their start and end apart: 23 -> 22, of which waited for: 13 -> 13; matrix products, arithmetic and copies ran while one was open for 0% -> 0% of each run, Pallas kernels for 3% -> 2%
where the time goes in v3:
time: 110 us
  waiting for transfers between devices  64.9 us (59%)
  starting transfers between devices  38.7 us (35%)
  Pallas kernels  6.08 us (6%)
    ppermute x19, waiting for transfers between devices, send(): return lax.ppermute(x, 'wide', pairs)  59.1 us
    ppermute x19, starting transfers between devices, send(): return lax.ppermute(x, 'wide', pairs)  35.2 us
    ppermute x3, waiting for transfers between devices, folded(): lax.ppermute(here, 'narrow', [(i, i ^ d) for i in range(LINE)])  5.79 us
    ppermute x3, starting transfers between devices, folded(): lax.ppermute(here, 'narrow', [(i, i ^ d) for i in range(LINE)])  3.55 us
    pallas_call x1, Pallas kernels, cut(): pl.pallas_call(functools.partial(cut_kernel, start, size), in_specs=[in_h...  2.39 us
  transfers between devices with their start and end apart: 22, of which 13 were waited for; matrix products, arithmetic and copies ran while one was open for 0% of the time, Pallas kernels for 2%

profile of v3, /device:TPU:0, one launch (start us, length us, event | category | flops | bytes accessed | tf_op | source)
XLA Modules:
  0.0 110.0 jit_solution(6205964337599548819)
XLA Ops:
  0.0 0.0 copy-start
  0.0 0.0 copy-start.1
  0.0 2.4 %cut.1 = bf16[3712,128]{1,0:T(8,128)(2,1)} custom-call(bf16[3696,128]{1,0:T(8,128)(2,1)} %bitcast.3, bf16[3696,128]{1,0:T(8,128)(2,1)} %bitcast.6), custom_call_target="tpu_custom_call" | custom-call | bytes 1892352 | tf_op jit(solution)/shard_map/cut/pallas_call | solution.py:76
  2.4 0.0 copy-start.2
  2.4 0.5 collective-permute-start
  2.9 2.4 %collective-permute-done.got_ref = bf16[3712,128]{1,0:T(8,128)(2,1)S(1)} collective-permute-done((bf16[3712,128]{1,0:T(8,128)(2,1)}, bf16[3712,128]{1,0:T(8,128)(2,1)S(1)}, u32[]{:S(2)}, u32[]{:S(2)}) %collective-permute-start) | collective-permute-done | bytes 950304 | tf_op jit(solution)/shard_map/swap/ppermute | solution.py:326
  5.3 0.0 copy-done
  5.3 0.0 copy-done.1
  5.3 0.5 pack.2
  5.8 4.9 %collective-permute-start.7 = (bf16[1408,256]{1,0:T(8,128)(2,1)S(1)}, bf16[1408,256]{1,0:T(8,128)(2,1)S(1)}, u32[]{:S(2)}, u32[]{:S(2)}) collective-permute-start(bf16[1408,256]{1,0:T(8,128)(2,1)S(1)} %get-tuple-element.31), channel_id=1, source_target_pairs={{0,8},{4,12},{24,16},{28,20},{1,9},{5,13},{25,17},{29,21},{2,10},{... | collective-permute-start | bytes 2162696 | tf_op jit(solution)/shard_map/outer_0/ppermute | solution.py:326
  10.7 0.8 collective-permute-start.6
  11.5 0.0 copy-done.2
  11.5 1.6 %collective-permute-start.1 = (bf16[256,256]{1,0:T(8,128)(2,1)S(1)}, bf16[256,256]{1,0:T(8,128)(2,1)S(1)}, u32[]{:S(2)}, u32[]{:S(2)}) collective-permute-start(bf16[256,256]{1,0:T(8,128)(2,1)S(1)} %copy-done.2), channel_id=1, source_target_pairs={{0,1},{1,0},{2,3},{3,2},{4,5},{5,4},{6,7},{7,6},{8,9},{9,8},{10,11... | collective-permute-start | bytes 393224 | tf_op jit(solution)/shard_map/ppermute | solution.py:346
  13.1 1.5 %collective-permute-start.2 = (bf16[256,256]{1,0:T(8,128)(2,1)S(1)}, bf16[256,256]{1,0:T(8,128)(2,1)S(1)}, u32[]{:S(2)}, u32[]{:S(2)}) collective-permute-start(bf16[256,256]{1,0:T(8,128)(2,1)S(1)} %copy-done.2), channel_id=1, source_target_pairs={{0,2},{1,3},{2,0},{3,1},{4,6},{5,7},{6,4},{7,5},{8,10},{9,11},{10,... | collective-permute-start | bytes 393224 | tf_op jit(solution)/shard_map/ppermute | solution.py:346
  14.6 0.5 collective-permute-start.3
  15.1 2.1 %collective-permute-done.1.refs_1_ = bf16[256,256]{1,0:T(8,128)(2,1)S(1)} collective-permute-done((bf16[256,256]{1,0:T(8,128)(2,1)S(1)}, bf16[256,256]{1,0:T(8,128)(2,1)S(1)}, u32[]{:S(2)}, u32[]{:S(2)}) %collective-permute-start.1) | collective-permute-done | bytes 131104 | tf_op jit(solution)/shard_map/ppermute | solution.py:346
  17.2 3.6 %collective-permute-done.2.refs_2_ = bf16[256,256]{1,0:T(8,128)(2,1)S(1)} collective-permute-done((bf16[256,256]{1,0:T(8,128)(2,1)S(1)}, bf16[256,256]{1,0:T(8,128)(2,1)S(1)}, u32[]{:S(2)}, u32[]{:S(2)}) %collective-permute-start.2) | collective-permute-done | bytes 131104 | tf_op jit(solution)/shard_map/ppermute | solution.py:346
  20.8 0.0 collective-permute-done.3.refs_3_
  20.8 0.2 arrange.1
  21.0 4.0 %collective-permute-start.4 = (bf16[1024,256]{1,0:T(8,128)(2,1)S(1)}, bf16[1024,256]{1,0:T(8,128)(2,1)S(1)}, u32[]{:S(2)}, u32[]{:S(2)}) collective-permute-start(bf16[1024,256]{1,0:T(8,128)(2,1)S(1)} %get-tuple-element.34), channel_id=1, source_target_pairs={{0,8},{4,12},{24,16},{28,20},{1,9},{5,13},{25,17},{29,21},{2,10},{... | collective-permute-start | bytes 1572872 | tf_op jit(solution)/shard_map/x_outer/ppermute | solution.py:326
  25.1 0.3 pack.3
  25.4 1.8 %collective-permute-done.7.refs_4_ = bf16[1408,256]{1,0:T(8,128)(2,1)S(1)} collective-permute-done((bf16[1408,256]{1,0:T(8,128)(2,1)S(1)}, bf16[1408,256]{1,0:T(8,128)(2,1)S(1)}, u32[]{:S(2)}, u32[]{:S(2)}) %collective-permute-start.7) | collective-permute-done | bytes 720928 | tf_op jit(solution)/shard_map/outer_0/ppermute | solution.py:326
  27.2 4.4 %collective-permute-start.10 = (bf16[1536,256]{1,0:T(8,128)(2,1)S(1)}, bf16[1536,256]{1,0:T(8,128)(2,1)S(1)}, u32[]{:S(2)}, u32[]{:S(2)}) collective-permute-start(bf16[1536,256]{1,0:T(8,128)(2,1)S(1)} %get-tuple-element.40), channel_id=1, source_target_pairs={{0,8},{4,12},{24,16},{28,20},{1,9},{5,13},{25,17},{29,21},{2,10},{... | collective-permute-start | bytes 2359304 | tf_op jit(solution)/shard_map/outer_1/ppermute | solution.py:326
  31.6 6.8 %collective-permute-done.4.refs_0_ = bf16[1024,256]{1,0:T(8,128)(2,1)S(1)} collective-permute-done((bf16[1024,256]{1,0:T(8,128)(2,1)S(1)}, bf16[1024,256]{1,0:T(8,128)(2,1)S(1)}, u32[]{:S(2)}, u32[]{:S(2)}) %collective-permute-start.4) | collective-permute-done | bytes 524320 | tf_op jit(solution)/shard_map/x_outer/ppermute | solution.py:326
  38.4 0.0 collective-permute-start.5
  38.4 0.7 collective-permute-start.8
  39.1 1.2 %collective-permute-done.5.refs_1_ = bf16[1024,256]{1,0:T(8,128)(2,1)S(1)} collective-permute-done((bf16[1024,256]{1,0:T(8,128)(2,1)S(1)}, bf16[1024,256]{1,0:T(8,128)(2,1)S(1)}, u32[]{:S(2)}, u32[]{:S(2)}) %collective-permute-start.5) | collective-permute-done | bytes 524320 | tf_op jit(solution)/shard_map/x_outer_other/ppermute | solution.py:326
  40.3 0.0 collective-permute-done.6.refs_3_
  40.3 14.1 %collective-permute-done.10.refs_4_ = bf16[1536,256]{1,0:T(8,128)(2,1)S(1)} collective-permute-done((bf16[1536,256]{1,0:T(8,128)(2,1)S(1)}, bf16[1536,256]{1,0:T(8,128)(2,1)S(1)}, u32[]{:S(2)}, u32[]{:S(2)}) %collective-permute-start.10) | collective-permute-done | bytes 786464 | tf_op jit(solution)/shard_map/outer_1/ppermute | solution.py:326
  54.4 0.7 collective-permute-start.11
  55.2 0.1 collective-permute-start.9
  55.2 0.0 collective-permute-done.8.refs_5_
  55.3 1.3 %collective-permute-start.16 = (bf16[704,512]{1,0:T(8,128)(2,1)S(1)}, bf16[704,512]{1,0:T(8,128)(2,1)S(1)}, u32[]{:S(2)}, u32[]{:S(2)}) collective-permute-start(bf16[704,512]{1,0:T(8,128)(2,1)S(1)} %outer_hidden.3), channel_id=1, source_target_pairs={{8,0},{12,4},{16,24},{20,28},{9,1},{13,5},{17,25},{21,29},{10,2},{... | collective-permute-start | bytes 2162696 | tf_op jit(solution)/shard_map/back_0/ppermute | solution.py:326
  56.6 11.6 %collective-permute-start.13 = (bf16[768,256]{1,0:T(8,128)(2,1)S(1)}, bf16[768,256]{1,0:T(8,128)(2,1)S(1)}, u32[]{:S(2)}, u32[]{:S(2)}) collective-permute-start(bf16[768,256]{1,0:T(8,128)(2,1)S(1)} %get-tuple-element.45.refs_2_), channel_id=1, source_target_pairs={{0,8},{4,12},{24,16},{28,20},{1,9},{5,13},{25,17},{29,21},{2,10},{... | collective-permute-start | bytes 1179656 | tf_op jit(solution)/shard_map/outer_2/ppermute | solution.py:326
  68.2 0.7 collective-permute-start.12
  68.9 0.0 collective-permute-done.9.refs_1_
  68.9 0.1 own_hidden.3
  68.9 0.0 collective-permute-done.11.refs_5_
  69.0 1.3 %collective-permute-start.18 = (bf16[768,512]{1,0:T(8,128)(2,1)S(1)}, bf16[768,512]{1,0:T(8,128)(2,1)S(1)}, u32[]{:S(2)}, u32[]{:S(2)}) collective-permute-start(bf16[768,512]{1,0:T(8,128)(2,1)S(1)} %outer_hidden.4), channel_id=1, source_target_pairs={{8,0},{12,4},{16,24},{20,28},{9,1},{13,5},{17,25},{21,29},{10,2},{... | collective-permute-start | bytes 2359304 | tf_op jit(solution)/shard_map/back_1/ppermute | solution.py:326
  70.3 0.1 collective-permute-start.15
  70.4 4.8 %collective-permute-done.13.refs_4_ = bf16[768,256]{1,0:T(8,128)(2,1)S(1)} collective-permute-done((bf16[768,256]{1,0:T(8,128)(2,1)S(1)}, bf16[768,256]{1,0:T(8,128)(2,1)S(1)}, u32[]{:S(2)}, u32[]{:S(2)}) %collective-permute-start.13) | collective-permute-done | bytes 393248 | tf_op jit(solution)/shard_map/outer_2/ppermute | solution.py:326
  75.2 0.7 collective-permute-start.14
  75.9 0.0 collective-permute-done.12.refs_3_
  75.9 0.0 collective-permute-done.15.refs_6_
  75.9 5.1 %collective-permute-done.16.refs_7_ = bf16[704,512]{1,0:T(8,128)(2,1)S(1)} collective-permute-done((bf16[704,512]{1,0:T(8,128)(2,1)S(1)}, bf16[704,512]{1,0:T(8,128)(2,1)S(1)}, u32[]{:S(2)}, u32[]{:S(2)}) %collective-permute-start.16) | collective-permute-done | bytes 720928 | tf_op jit(solution)/shard_map/back_0/ppermute | solution.py:326
  81.0 0.8 own_hidden.4
  81.8 0.1 collective-permute-start.17
  81.8 0.0 collective-permute-done.14.refs_5_
  81.9 1.3 %collective-permute-start.19 = (bf16[384,256]{1,0:T(8,128)(2,1)S(1)}, bf16[384,256]{1,0:T(8,128)(2,1)S(1)}, u32[]{:S(2)}, u32[]{:S(2)}) collective-permute-start(bf16[384,256]{1,0:T(8,128)(2,1)S(1)} %get-tuple-element.47), channel_id=1, source_target_pairs={{8,0},{12,4},{16,24},{20,28},{9,1},{13,5},{17,25},{21,29},{10,2},{... | collective-permute-start | bytes 589832 | tf_op jit(solution)/shard_map/back_2_same/ppermute | solution.py:326
  83.2 1.3 %collective-permute-start.20 = (bf16[384,256]{1,0:T(8,128)(2,1)S(1)}, bf16[384,256]{1,0:T(8,128)(2,1)S(1)}, u32[]{:S(2)}, u32[]{:S(2)}) collective-permute-start(bf16[384,256]{1,0:T(8,128)(2,1)S(1)} %get-tuple-element.54), channel_id=1, source_target_pairs={{8,4},{12,0},{16,28},{20,24},{9,5},{13,1},{17,29},{21,25},{10,6},{... | collective-permute-start | bytes 589832 | tf_op jit(solution)/shard_map/back_2_cross/ppermute | solution.py:326
  84.5 0.0 collective-permute-done.17.refs_6_
  84.5 14.9 %collective-permute-done.18.refs_7_ = bf16[768,512]{1,0:T(8,128)(2,1)S(1)} collective-permute-done((bf16[768,512]{1,0:T(8,128)(2,1)S(1)}, bf16[768,512]{1,0:T(8,128)(2,1)S(1)}, u32[]{:S(2)}, u32[]{:S(2)}) %collective-permute-start.18) | collective-permute-done | bytes 786464 | tf_op jit(solution)/shard_map/back_1/ppermute | solution.py:326
  99.4 0.9 own_hidden.5
  100.3 4.5 %collective-permute-done.19.refs_1_ = bf16[384,256]{1,0:T(8,128)(2,1)S(1)} collective-permute-done((bf16[384,256]{1,0:T(8,128)(2,1)S(1)}, bf16[384,256]{1,0:T(8,128)(2,1)S(1)}, u32[]{:S(2)}, u32[]{:S(2)}) %collective-permute-start.19) | collective-permute-done | bytes 196640 | tf_op jit(solution)/shard_map/back_2_same/ppermute | solution.py:326
  104.7 2.2 %collective-permute-done.20.refs_2_ = bf16[384,256]{1,0:T(8,128)(2,1)S(1)} collective-permute-done((bf16[384,256]{1,0:T(8,128)(2,1)S(1)}, bf16[384,256]{1,0:T(8,128)(2,1)S(1)}, u32[]{:S(2)}, u32[]{:S(2)}) %collective-permute-start.20) | collective-permute-done | bytes 196640 | tf_op jit(solution)/shard_map/back_2_cross/ppermute | solution.py:326
  107.0 0.8 collective-permute-start.21
  107.8 1.3 %collective-permute-done.21.refs_0_ = bf16[768,256]{1,0:T(8,128)(2,1)S(1)} collective-permute-done((bf16[768,256]{1,0:T(8,128)(2,1)S(1)}, bf16[768,256]{1,0:T(8,128)(2,1)S(1)}, u32[]{:S(2)}, u32[]{:S(2)}) %collective-permute-start.21) | collective-permute-done | bytes 393248 | tf_op jit(solution)/shard_map/swapped_2/ppermute | solution.py:326
  109.1 0.9 put.1
  (3 shorter events, 0.1 us)
Async XLA Ops:
  0.0 5.3 %copy-start = (bf16[128,3696]{0,1:T(8,128)(2,1)S(1)}, bf16[128,3696]{0,1:T(8,128)(2,1)}, u32[]{:S(2)}) copy-start(bf16[128,3696]{0,1:T(8,128)(2,1)} %param.4) | copy-start | bytes 2838532
  0.0 5.3 %copy-start.1 = (bf16[128,3696]{0,1:T(8,128)(2,1)S(1)}, bf16[128,3696]{0,1:T(8,128)(2,1)}, u32[]{:S(2)}) copy-start(bf16[128,3696]{0,1:T(8,128)(2,1)} %param.5) | copy-start | bytes 2838532
  2.4 9.1 %copy-start.2 = (bf16[256,256]{1,0:T(8,128)(2,1)S(1)}, bf16[256,256]{1,0:T(8,128)(2,1)}, u32[]{:S(2)}) copy-start(bf16[256,256]{1,0:T(8,128)(2,1)} %refs_0_) | copy-start | bytes 393220
  2.4 2.9 %collective-permute-start = (bf16[3712,128]{1,0:T(8,128)(2,1)}, bf16[3712,128]{1,0:T(8,128)(2,1)S(1)}, u32[]{:S(2)}, u32[]{:S(2)}) collective-permute-start(bf16[3712,128]{1,0:T(8,128)(2,1)} %cut.1), channel_id=1, source_target_pairs={{0,4},{4,0},{8,12},{12,8},{16,20},{20,16},{24,28},{28,24},{1,5},{5... | collective-permute-start | bytes 2850824 | tf_op jit(solution)/shard_map/swap/ppermute | solution.py:326
  5.8 21.3 %collective-permute-start.7 = (bf16[1408,256]{1,0:T(8,128)(2,1)S(1)}, bf16[1408,256]{1,0:T(8,128)(2,1)S(1)}, u32[]{:S(2)}, u32[]{:S(2)}) collective-permute-start(bf16[1408,256]{1,0:T(8,128)(2,1)S(1)} %get-tuple-element.31), channel_id=1, source_target_pairs={{0,8},{4,12},{24,16},{28,20},{1,9},{5,13},{25,17},{29,21},{2,10},{... | collective-permute-start | bytes 2162696 | tf_op jit(solution)/shard_map/outer_0/ppermute | solution.py:326
  10.7 29.6 %collective-permute-start.6 = (bf16[2944,256]{1,0:T(8,128)(2,1)S(1)}, bf16[2944,256]{1,0:T(8,128)(2,1)S(1)}, u32[]{:S(2)}, u32[]{:S(2)}) collective-permute-start(bf16[2944,256]{1,0:T(8,128)(2,1)S(1)} %get-tuple-element.35.refs_2_), channel_id=1, source_target_pairs={{8,16},{12,20},{16,8},{20,12},{9,17},{13,21},{17,9},{21,13},{10,18... | collective-permute-start | bytes 4521992 | tf_op jit(solution)/shard_map/own_01/ppermute | solution.py:326
  11.5 5.7 %collective-permute-start.1 = (bf16[256,256]{1,0:T(8,128)(2,1)S(1)}, bf16[256,256]{1,0:T(8,128)(2,1)S(1)}, u32[]{:S(2)}, u32[]{:S(2)}) collective-permute-start(bf16[256,256]{1,0:T(8,128)(2,1)S(1)} %copy-done.2), channel_id=1, source_target_pairs={{0,1},{1,0},{2,3},{3,2},{4,5},{5,4},{6,7},{7,6},{8,9},{9,8},{10,11... | collective-permute-start | bytes 393224 | tf_op jit(solution)/shard_map/ppermute | solution.py:346
  13.1 7.8 %collective-permute-start.2 = (bf16[256,256]{1,0:T(8,128)(2,1)S(1)}, bf16[256,256]{1,0:T(8,128)(2,1)S(1)}, u32[]{:S(2)}, u32[]{:S(2)}) collective-permute-start(bf16[256,256]{1,0:T(8,128)(2,1)S(1)} %copy-done.2), channel_id=1, source_target_pairs={{0,2},{1,3},{2,0},{3,1},{4,6},{5,7},{6,4},{7,5},{8,10},{9,11},{10,... | collective-permute-start | bytes 393224 | tf_op jit(solution)/shard_map/ppermute | solution.py:346
  14.6 6.3 %collective-permute-start.3 = (bf16[256,256]{1,0:T(8,128)(2,1)S(1)}, bf16[256,256]{1,0:T(8,128)(2,1)S(1)}, u32[]{:S(2)}, u32[]{:S(2)}) collective-permute-start(bf16[256,256]{1,0:T(8,128)(2,1)S(1)} %copy-done.2), channel_id=1, source_target_pairs={{0,3},{1,2},{2,1},{3,0},{4,7},{5,6},{6,5},{7,4},{8,11},{9,10},{10,... | collective-permute-start | bytes 393224 | tf_op jit(solution)/shard_map/ppermute | solution.py:346
  21.0 17.4 %collective-permute-start.4 = (bf16[1024,256]{1,0:T(8,128)(2,1)S(1)}, bf16[1024,256]{1,0:T(8,128)(2,1)S(1)}, u32[]{:S(2)}, u32[]{:S(2)}) collective-permute-start(bf16[1024,256]{1,0:T(8,128)(2,1)S(1)} %get-tuple-element.34), channel_id=1, source_target_pairs={{0,8},{4,12},{24,16},{28,20},{1,9},{5,13},{25,17},{29,21},{2,10},{... | collective-permute-start | bytes 1572872 | tf_op jit(solution)/shard_map/x_outer/ppermute | solution.py:326
  27.2 27.3 %collective-permute-start.10 = (bf16[1536,256]{1,0:T(8,128)(2,1)S(1)}, bf16[1536,256]{1,0:T(8,128)(2,1)S(1)}, u32[]{:S(2)}, u32[]{:S(2)}) collective-permute-start(bf16[1536,256]{1,0:T(8,128)(2,1)S(1)} %get-tuple-element.40), channel_id=1, source_target_pairs={{0,8},{4,12},{24,16},{28,20},{1,9},{5,13},{25,17},{29,21},{2,10},{... | collective-permute-start | bytes 2359304 | tf_op jit(solution)/shard_map/outer_1/ppermute | solution.py:326
  38.4 1.9 %collective-permute-start.5 = (bf16[1024,256]{1,0:T(8,128)(2,1)S(1)}, bf16[1024,256]{1,0:T(8,128)(2,1)S(1)}, u32[]{:S(2)}, u32[]{:S(2)}) collective-permute-start(bf16[1024,256]{1,0:T(8,128)(2,1)S(1)} %collective-permute-done.4.refs_0_), channel_id=1, source_target_pairs={{0,4},{4,0},{8,12},{12,8},{16,20},{20,16},{24,28},{28,24},{1,5},{5... | collective-permute-start | bytes 1572872 | tf_op jit(solution)/shard_map/x_outer_other/ppermute | solution.py:326
  38.4 16.8 %collective-permute-start.8 = (bf16[1408,256]{1,0:T(8,128)(2,1)S(1)}, bf16[1408,256]{1,0:T(8,128)(2,1)S(1)}, u32[]{:S(2)}, u32[]{:S(2)}) collective-permute-start(bf16[1408,256]{1,0:T(8,128)(2,1)S(1)} %collective-permute-done.7.refs_4_), channel_id=1, source_target_pairs={{8,16},{12,20},{16,8},{20,12},{9,17},{13,21},{17,9},{21,13},{10,18... | collective-permute-start | bytes 2162696 | tf_op jit(solution)/shard_map/far_0/ppermute | solution.py:326
  54.4 14.5 %collective-permute-start.11 = (bf16[1536,256]{1,0:T(8,128)(2,1)S(1)}, bf16[1536,256]{1,0:T(8,128)(2,1)S(1)}, u32[]{:S(2)}, u32[]{:S(2)}) collective-permute-start(bf16[1536,256]{1,0:T(8,128)(2,1)S(1)} %collective-permute-done.10.refs_4_), channel_id=1, source_target_pairs={{8,16},{12,20},{16,8},{20,12},{9,17},{13,21},{17,9},{21,13},{10,18... | collective-permute-start | bytes 2359304 | tf_op jit(solution)/shard_map/far_1/ppermute | solution.py:326
  55.2 13.7 %collective-permute-start.9 = (bf16[1024,256]{1,0:T(8,128)(2,1)S(1)}, bf16[1024,256]{1,0:T(8,128)(2,1)S(1)}, u32[]{:S(2)}, u32[]{:S(2)}) collective-permute-start(bf16[1024,256]{1,0:T(8,128)(2,1)S(1)} %get-tuple-element.49.refs_0_), channel_id=1, source_target_pairs={{0,4},{4,0},{8,12},{12,8},{16,20},{20,16},{24,28},{28,24},{1,5},{5... | collective-permute-start | bytes 1572872 | tf_op jit(solution)/shard_map/x_other/ppermute | solution.py:326
  55.3 25.7 %collective-permute-start.16 = (bf16[704,512]{1,0:T(8,128)(2,1)S(1)}, bf16[704,512]{1,0:T(8,128)(2,1)S(1)}, u32[]{:S(2)}, u32[]{:S(2)}) collective-permute-start(bf16[704,512]{1,0:T(8,128)(2,1)S(1)} %outer_hidden.3), channel_id=1, source_target_pairs={{8,0},{12,4},{16,24},{20,28},{9,1},{13,5},{17,25},{21,29},{10,2},{... | collective-permute-start | bytes 2162696 | tf_op jit(solution)/shard_map/back_0/ppermute | solution.py:326
  56.6 18.6 %collective-permute-start.13 = (bf16[768,256]{1,0:T(8,128)(2,1)S(1)}, bf16[768,256]{1,0:T(8,128)(2,1)S(1)}, u32[]{:S(2)}, u32[]{:S(2)}) collective-permute-start(bf16[768,256]{1,0:T(8,128)(2,1)S(1)} %get-tuple-element.45.refs_2_), channel_id=1, source_target_pairs={{0,8},{4,12},{24,16},{28,20},{1,9},{5,13},{25,17},{29,21},{2,10},{... | collective-permute-start | bytes 1179656 | tf_op jit(solution)/shard_map/outer_2/ppermute | solution.py:326
  68.2 7.7 %collective-permute-start.12 = (bf16[768,256]{1,0:T(8,128)(2,1)S(1)}, bf16[768,256]{1,0:T(8,128)(2,1)S(1)}, u32[]{:S(2)}, u32[]{:S(2)}) collective-permute-start(bf16[768,256]{1,0:T(8,128)(2,1)S(1)} %get-tuple-element.45.refs_2_), channel_id=1, source_target_pairs={{8,16},{12,20},{16,8},{20,12},{9,17},{13,21},{17,9},{21,13},{10,18... | collective-permute-start | bytes 1179656 | tf_op jit(solution)/shard_map/own_2/ppermute | solution.py:326
  69.0 30.4 %collective-permute-start.18 = (bf16[768,512]{1,0:T(8,128)(2,1)S(1)}, bf16[768,512]{1,0:T(8,128)(2,1)S(1)}, u32[]{:S(2)}, u32[]{:S(2)}) collective-permute-start(bf16[768,512]{1,0:T(8,128)(2,1)S(1)} %outer_hidden.4), channel_id=1, source_target_pairs={{8,0},{12,4},{16,24},{20,28},{9,1},{13,5},{17,25},{21,29},{10,2},{... | collective-permute-start | bytes 2359304 | tf_op jit(solution)/shard_map/back_1/ppermute | solution.py:326
  70.3 5.6 %collective-permute-start.15 = (bf16[704,256]{1,0:T(8,128)(2,1)S(1)}, bf16[704,256]{1,0:T(8,128)(2,1)S(1)}, u32[]{:S(2)}, u32[]{:S(2)}) collective-permute-start(bf16[704,256]{1,0:T(8,128)(2,1)S(1)} %get-tuple-element.37), channel_id=1, source_target_pairs={{0,4},{4,0},{8,12},{12,8},{16,20},{20,16},{24,28},{28,24},{1,5},{5... | collective-permute-start | bytes 1081352 | tf_op jit(solution)/shard_map/swapped_0/ppermute | solution.py:326
  75.2 6.7 %collective-permute-start.14 = (bf16[768,256]{1,0:T(8,128)(2,1)S(1)}, bf16[768,256]{1,0:T(8,128)(2,1)S(1)}, u32[]{:S(2)}, u32[]{:S(2)}) collective-permute-start(bf16[768,256]{1,0:T(8,128)(2,1)S(1)} %collective-permute-done.13.refs_4_), channel_id=1, source_target_pairs={{8,16},{12,20},{16,8},{20,12},{9,17},{13,21},{17,9},{21,13},{10,18... | collective-permute-start | bytes 1179656 | tf_op jit(solution)/shard_map/far_2/ppermute | solution.py:326
  81.8 2.7 %collective-permute-start.17 = (bf16[768,256]{1,0:T(8,128)(2,1)S(1)}, bf16[768,256]{1,0:T(8,128)(2,1)S(1)}, u32[]{:S(2)}, u32[]{:S(2)}) collective-permute-start(bf16[768,256]{1,0:T(8,128)(2,1)S(1)} %get-tuple-element.51), channel_id=1, source_target_pairs={{0,4},{4,0},{8,12},{12,8},{16,20},{20,16},{24,28},{28,24},{1,5},{5... | collective-permute-start | bytes 1179656 | tf_op jit(solution)/shard_map/swapped_1/ppermute | solution.py:326
  81.9 22.8 %collective-permute-start.19 = (bf16[384,256]{1,0:T(8,128)(2,1)S(1)}, bf16[384,256]{1,0:T(8,128)(2,1)S(1)}, u32[]{:S(2)}, u32[]{:S(2)}) collective-permute-start(bf16[384,256]{1,0:T(8,128)(2,1)S(1)} %get-tuple-element.47), channel_id=1, source_target_pairs={{8,0},{12,4},{16,24},{20,28},{9,1},{13,5},{17,25},{21,29},{10,2},{... | collective-permute-start | bytes 589832 | tf_op jit(solution)/shard_map/back_2_same/ppermute | solution.py:326
  83.2 23.8 %collective-permute-start.20 = (bf16[384,256]{1,0:T(8,128)(2,1)S(1)}, bf16[384,256]{1,0:T(8,128)(2,1)S(1)}, u32[]{:S(2)}, u32[]{:S(2)}) collective-permute-start(bf16[384,256]{1,0:T(8,128)(2,1)S(1)} %get-tuple-element.54), channel_id=1, source_target_pairs={{8,4},{12,0},{16,28},{20,24},{9,5},{13,1},{17,29},{21,25},{10,6},{... | collective-permute-start | bytes 589832 | tf_op jit(solution)/shard_map/back_2_cross/ppermute | solution.py:326
  107.0 2.2 %collective-permute-start.21 = (bf16[768,256]{1,0:T(8,128)(2,1)S(1)}, bf16[768,256]{1,0:T(8,128)(2,1)S(1)}, u32[]{:S(2)}, u32[]{:S(2)}) collective-permute-start(bf16[768,256]{1,0:T(8,128)(2,1)S(1)} %get-tuple-element.55), channel_id=1, source_target_pairs={{0,4},{4,0},{8,12},{12,8},{16,20},{20,16},{24,28},{28,24},{1,5},{5... | collective-permute-start | bytes 1179656 | tf_op jit(solution)/shard_map/swapped_2/ppermute | solution.py:326

commit v4 on v3

--- a/solution.py
+++ b/solution.py
@@ -332,9 +332,13 @@
     chunks = [(sum(n[:i]), n[i]) for i in range(3)]
 
     mine = gate_weight.T, up_weight.T
-    got = send(cut(*mine, 0, sum(n), LARGE), other_core, "swap")
+    first = n[0] + n[1]
+    got = send(cut(*mine, 0, first, LARGE), other_core, "swap")
     pack_01, pack_0 = pack(*mine, got, 0, chunks, ((0, 1), (0,)))
-    pack_1, pack_2 = pack(*mine, got, 0, chunks, ((1,), (2,)))
+    (pack_1,) = pack(*mine, got, 0, chunks, ((1,),))
+    rest = [after(w, pack_0) for w in mine]
+    got_rest = send(cut(*rest, first, n[2], SMALL), other_core, "swap_rest")
+    (pack_2,) = pack(*mine, got_rest, first, chunks, ((2,),))
 
     own_01 = send(pack_01, across, "own_01")
     outer_0 = send(pack_0, inward, "outer_0")

time: 110 us -> 110 us (level)
    ppermute x19 -> x20, waiting for transfers between devices: 59.1 us -> 58.8 us  [send(): return lax.ppermute(x, 'wide', pairs)]
    ppermute x19 -> x20, starting transfers between devices: 35.2 us -> 34.8 us  [send(): return lax.ppermute(x, 'wide', pairs)]
    pallas_call x1 -> x2, Pallas kernels: 2.39 us -> 2.62 us  [cut(): pl.pallas_call(functools.partial(cut_kernel, start, size), in_specs=[in_h...]
  transfers between devices with their start and end apart: 22 -> 23, of which waited for: 13 -> 13; matrix products, arithmetic and copies ran while one was open for 0% -> 0% of each run, Pallas kernels for 2% -> 2%
where the time goes in v4:
time: 110 us
  waiting for transfers between devices  64.6 us (59%)
  starting transfers between devices  38.4 us (35%)
  Pallas kernels  6.31 us (6%)
    ppermute x20, waiting for transfers between devices, send(): return lax.ppermute(x, 'wide', pairs)  58.8 us
    ppermute x20, starting transfers between devices, send(): return lax.ppermute(x, 'wide', pairs)  34.8 us
    ppermute x3, waiting for transfers between devices, folded(): lax.ppermute(here, 'narrow', [(i, i ^ d) for i in range(LINE)])  5.79 us
    ppermute x3, starting transfers between devices, folded(): lax.ppermute(here, 'narrow', [(i, i ^ d) for i in range(LINE)])  3.55 us
    pallas_call x2, Pallas kernels, cut(): pl.pallas_call(functools.partial(cut_kernel, start, size), in_specs=[in_h...  2.62 us
  transfers between devices with their start and end apart: 23, of which 13 were waited for; matrix products, arithmetic and copies ran while one was open for 0% of the time, Pallas kernels for 2%

profile of v4, /device:TPU:0, one launch (start us, length us, event | category | flops | bytes accessed | tf_op | source)
XLA Modules:
  0.0 109.6 jit_solution(11631506797475568528)
XLA Ops:
  0.0 0.0 copy-start
  0.0 0.0 copy-start.1
  0.0 2.3 %cut.2 = bf16[2944,128]{1,0:T(8,128)(2,1)} custom-call(bf16[3696,128]{1,0:T(8,128)(2,1)} %bitcast.3, bf16[3696,128]{1,0:T(8,128)(2,1)} %bitcast.8), custom_call_target="tpu_custom_call" | custom-call | bytes 1892352 | tf_op jit(solution)/shard_map/cut/pallas_call | solution.py:76
  2.3 0.0 copy-start.2
  2.3 0.5 collective-permute-start
  2.8 2.1 %collective-permute-done.got_ref = bf16[2944,128]{1,0:T(8,128)(2,1)S(1)} collective-permute-done((bf16[2944,128]{1,0:T(8,128)(2,1)}, bf16[2944,128]{1,0:T(8,128)(2,1)S(1)}, u32[]{:S(2)}, u32[]{:S(2)}) %collective-permute-start) | collective-permute-done | bytes 753696 | tf_op jit(solution)/shard_map/swap/ppermute | solution.py:326
  4.9 0.0 copy-done
  4.9 0.0 copy-done.1
  4.9 0.5 pack.3
  5.4 4.9 %collective-permute-start.7 = (bf16[1408,256]{1,0:T(8,128)(2,1)S(1)}, bf16[1408,256]{1,0:T(8,128)(2,1)S(1)}, u32[]{:S(2)}, u32[]{:S(2)}) collective-permute-start(bf16[1408,256]{1,0:T(8,128)(2,1)S(1)} %get-tuple-element.31), channel_id=1, source_target_pairs={{0,8},{4,12},{24,16},{28,20},{1,9},{5,13},{25,17},{29,21},{2,10},{... | collective-permute-start | bytes 2162696 | tf_op jit(solution)/shard_map/outer_0/ppermute | solution.py:326
  10.3 0.8 collective-permute-start.6
  11.1 0.0 copy-done.2
  11.1 1.6 %collective-permute-start.1 = (bf16[256,256]{1,0:T(8,128)(2,1)S(1)}, bf16[256,256]{1,0:T(8,128)(2,1)S(1)}, u32[]{:S(2)}, u32[]{:S(2)}) collective-permute-start(bf16[256,256]{1,0:T(8,128)(2,1)S(1)} %copy-done.2), channel_id=1, source_target_pairs={{0,1},{1,0},{2,3},{3,2},{4,5},{5,4},{6,7},{7,6},{8,9},{9,8},{10,11... | collective-permute-start | bytes 393224 | tf_op jit(solution)/shard_map/ppermute | solution.py:350
  12.6 1.5 %collective-permute-start.2 = (bf16[256,256]{1,0:T(8,128)(2,1)S(1)}, bf16[256,256]{1,0:T(8,128)(2,1)S(1)}, u32[]{:S(2)}, u32[]{:S(2)}) collective-permute-start(bf16[256,256]{1,0:T(8,128)(2,1)S(1)} %copy-done.2), channel_id=1, source_target_pairs={{0,2},{1,3},{2,0},{3,1},{4,6},{5,7},{6,4},{7,5},{8,10},{9,11},{10,... | collective-permute-start | bytes 393224 | tf_op jit(solution)/shard_map/ppermute | solution.py:350
  14.2 0.5 collective-permute-start.3
  14.6 2.1 %collective-permute-done.1.refs_1_ = bf16[256,256]{1,0:T(8,128)(2,1)S(1)} collective-permute-done((bf16[256,256]{1,0:T(8,128)(2,1)S(1)}, bf16[256,256]{1,0:T(8,128)(2,1)S(1)}, u32[]{:S(2)}, u32[]{:S(2)}) %collective-permute-start.1) | collective-permute-done | bytes 131104 | tf_op jit(solution)/shard_map/ppermute | solution.py:350
  16.8 3.6 %collective-permute-done.2.refs_2_ = bf16[256,256]{1,0:T(8,128)(2,1)S(1)} collective-permute-done((bf16[256,256]{1,0:T(8,128)(2,1)S(1)}, bf16[256,256]{1,0:T(8,128)(2,1)S(1)}, u32[]{:S(2)}, u32[]{:S(2)}) %collective-permute-start.2) | collective-permute-done | bytes 131104 | tf_op jit(solution)/shard_map/ppermute | solution.py:350
  20.4 0.0 collective-permute-done.3.refs_3_
  20.4 0.2 arrange.1
  20.6 4.0 %collective-permute-start.4 = (bf16[1024,256]{1,0:T(8,128)(2,1)S(1)}, bf16[1024,256]{1,0:T(8,128)(2,1)S(1)}, u32[]{:S(2)}, u32[]{:S(2)}) collective-permute-start(bf16[1024,256]{1,0:T(8,128)(2,1)S(1)} %get-tuple-element.34), channel_id=1, source_target_pairs={{0,8},{4,12},{24,16},{28,20},{1,9},{5,13},{25,17},{29,21},{2,10},{... | collective-permute-start | bytes 1572872 | tf_op jit(solution)/shard_map/x_outer/ppermute | solution.py:326
  24.6 0.2 pack.4
  24.9 1.9 %collective-permute-done.7.refs_4_ = bf16[1408,256]{1,0:T(8,128)(2,1)S(1)} collective-permute-done((bf16[1408,256]{1,0:T(8,128)(2,1)S(1)}, bf16[1408,256]{1,0:T(8,128)(2,1)S(1)}, u32[]{:S(2)}, u32[]{:S(2)}) %collective-permute-start.7) | collective-permute-done | bytes 720928 | tf_op jit(solution)/shard_map/outer_0/ppermute | solution.py:326
  26.8 4.4 %collective-permute-start.10 = (bf16[1536,256]{1,0:T(8,128)(2,1)S(1)}, bf16[1536,256]{1,0:T(8,128)(2,1)S(1)}, u32[]{:S(2)}, u32[]{:S(2)}) collective-permute-start(bf16[1536,256]{1,0:T(8,128)(2,1)S(1)} %pack.4), channel_id=1, source_target_pairs={{0,8},{4,12},{24,16},{28,20},{1,9},{5,13},{25,17},{29,21},{2,10},{... | collective-permute-start | bytes 2359304 | tf_op jit(solution)/shard_map/outer_1/ppermute | solution.py:326
  31.2 6.8 %collective-permute-done.4.refs_0_ = bf16[1024,256]{1,0:T(8,128)(2,1)S(1)} collective-permute-done((bf16[1024,256]{1,0:T(8,128)(2,1)S(1)}, bf16[1024,256]{1,0:T(8,128)(2,1)S(1)}, u32[]{:S(2)}, u32[]{:S(2)}) %collective-permute-start.4) | collective-permute-done | bytes 524320 | tf_op jit(solution)/shard_map/x_outer/ppermute | solution.py:326
  38.0 0.0 collective-permute-start.5
  38.0 0.7 collective-permute-start.8
  38.7 1.2 %collective-permute-done.5.refs_1_ = bf16[1024,256]{1,0:T(8,128)(2,1)S(1)} collective-permute-done((bf16[1024,256]{1,0:T(8,128)(2,1)S(1)}, bf16[1024,256]{1,0:T(8,128)(2,1)S(1)}, u32[]{:S(2)}, u32[]{:S(2)}) %collective-permute-start.5) | collective-permute-done | bytes 524320 | tf_op jit(solution)/shard_map/x_outer_other/ppermute | solution.py:326
  39.9 0.0 collective-permute-done.6.refs_3_
  39.9 14.1 %collective-permute-done.10.refs_4_ = bf16[1536,256]{1,0:T(8,128)(2,1)S(1)} collective-permute-done((bf16[1536,256]{1,0:T(8,128)(2,1)S(1)}, bf16[1536,256]{1,0:T(8,128)(2,1)S(1)}, u32[]{:S(2)}, u32[]{:S(2)}) %collective-permute-start.10) | collective-permute-done | bytes 786464 | tf_op jit(solution)/shard_map/outer_1/ppermute | solution.py:326
  54.0 0.7 collective-permute-start.11
  54.7 0.1 collective-permute-start.9
  54.8 0.4 cut.3
  55.2 0.5 collective-permute-start.12
  55.7 0.0 collective-permute-done.8.refs_5_
  55.7 1.3 %collective-permute-start.17 = (bf16[704,512]{1,0:T(8,128)(2,1)S(1)}, bf16[704,512]{1,0:T(8,128)(2,1)S(1)}, u32[]{:S(2)}, u32[]{:S(2)}) collective-permute-start(bf16[704,512]{1,0:T(8,128)(2,1)S(1)} %outer_hidden.3), channel_id=1, source_target_pairs={{8,0},{12,4},{16,24},{20,28},{9,1},{13,5},{17,25},{21,29},{10,2},{... | collective-permute-start | bytes 2162696 | tf_op jit(solution)/shard_map/back_0/ppermute | solution.py:326
  57.0 0.0 collective-permute-done.12.got_ref
  57.0 0.1 pack.5.refs_2_
  57.2 10.8 %collective-permute-start.14 = (bf16[768,256]{1,0:T(8,128)(2,1)S(1)}, bf16[768,256]{1,0:T(8,128)(2,1)S(1)}, u32[]{:S(2)}, u32[]{:S(2)}) collective-permute-start(bf16[768,256]{1,0:T(8,128)(2,1)S(1)} %pack.5.refs_2_), channel_id=1, source_target_pairs={{0,8},{4,12},{24,16},{28,20},{1,9},{5,13},{25,17},{29,21},{2,10},{... | collective-permute-start | bytes 1179656 | tf_op jit(solution)/shard_map/outer_2/ppermute | solution.py:326
  67.9 0.7 collective-permute-start.13
  68.6 0.0 collective-permute-done.9.refs_1_
  68.7 0.1 own_hidden.3
  68.7 0.0 collective-permute-done.11.refs_5_
  68.8 1.3 %collective-permute-start.19 = (bf16[768,512]{1,0:T(8,128)(2,1)S(1)}, bf16[768,512]{1,0:T(8,128)(2,1)S(1)}, u32[]{:S(2)}, u32[]{:S(2)}) collective-permute-start(bf16[768,512]{1,0:T(8,128)(2,1)S(1)} %outer_hidden.4), channel_id=1, source_target_pairs={{8,0},{12,4},{16,24},{20,28},{9,1},{13,5},{17,25},{21,29},{10,2},{... | collective-permute-start | bytes 2359304 | tf_op jit(solution)/shard_map/back_1/ppermute | solution.py:326
  70.1 0.1 collective-permute-start.16
  70.1 4.8 %collective-permute-done.14.refs_4_ = bf16[768,256]{1,0:T(8,128)(2,1)S(1)} collective-permute-done((bf16[768,256]{1,0:T(8,128)(2,1)S(1)}, bf16[768,256]{1,0:T(8,128)(2,1)S(1)}, u32[]{:S(2)}, u32[]{:S(2)}) %collective-permute-start.14) | collective-permute-done | bytes 393248 | tf_op jit(solution)/shard_map/outer_2/ppermute | solution.py:326
  75.0 0.7 collective-permute-start.15
  75.6 0.0 collective-permute-done.13.refs_3_
  75.6 0.0 collective-permute-done.16.refs_6_
  75.7 4.9 %collective-permute-done.17.refs_7_ = bf16[704,512]{1,0:T(8,128)(2,1)S(1)} collective-permute-done((bf16[704,512]{1,0:T(8,128)(2,1)S(1)}, bf16[704,512]{1,0:T(8,128)(2,1)S(1)}, u32[]{:S(2)}, u32[]{:S(2)}) %collective-permute-start.17) | collective-permute-done | bytes 720928 | tf_op jit(solution)/shard_map/back_0/ppermute | solution.py:326
  80.6 0.8 own_hidden.4
  81.4 0.1 collective-permute-start.18
  81.5 0.0 collective-permute-done.15.refs_5_
  81.5 1.3 %collective-permute-start.20 = (bf16[384,256]{1,0:T(8,128)(2,1)S(1)}, bf16[384,256]{1,0:T(8,128)(2,1)S(1)}, u32[]{:S(2)}, u32[]{:S(2)}) collective-permute-start(bf16[384,256]{1,0:T(8,128)(2,1)S(1)} %get-tuple-element.47), channel_id=1, source_target_pairs={{8,0},{12,4},{16,24},{20,28},{9,1},{13,5},{17,25},{21,29},{10,2},{... | collective-permute-start | bytes 589832 | tf_op jit(solution)/shard_map/back_2_same/ppermute | solution.py:326
  82.8 1.3 %collective-permute-start.21 = (bf16[384,256]{1,0:T(8,128)(2,1)S(1)}, bf16[384,256]{1,0:T(8,128)(2,1)S(1)}, u32[]{:S(2)}, u32[]{:S(2)}) collective-permute-start(bf16[384,256]{1,0:T(8,128)(2,1)S(1)} %get-tuple-element.54), channel_id=1, source_target_pairs={{8,4},{12,0},{16,28},{20,24},{9,5},{13,1},{17,29},{21,25},{10,6},{... | collective-permute-start | bytes 589832 | tf_op jit(solution)/shard_map/back_2_cross/ppermute | solution.py:326
  84.1 0.0 collective-permute-done.18.refs_6_
  84.1 14.9 %collective-permute-done.19.refs_7_ = bf16[768,512]{1,0:T(8,128)(2,1)S(1)} collective-permute-done((bf16[768,512]{1,0:T(8,128)(2,1)S(1)}, bf16[768,512]{1,0:T(8,128)(2,1)S(1)}, u32[]{:S(2)}, u32[]{:S(2)}) %collective-permute-start.19) | collective-permute-done | bytes 786464 | tf_op jit(solution)/shard_map/back_1/ppermute | solution.py:326
  99.0 0.9 own_hidden.5
  99.9 4.5 %collective-permute-done.20.refs_1_ = bf16[384,256]{1,0:T(8,128)(2,1)S(1)} collective-permute-done((bf16[384,256]{1,0:T(8,128)(2,1)S(1)}, bf16[384,256]{1,0:T(8,128)(2,1)S(1)}, u32[]{:S(2)}, u32[]{:S(2)}) %collective-permute-start.20) | collective-permute-done | bytes 196640 | tf_op jit(solution)/shard_map/back_2_same/ppermute | solution.py:326
  104.3 2.2 %collective-permute-done.21.refs_2_ = bf16[384,256]{1,0:T(8,128)(2,1)S(1)} collective-permute-done((bf16[384,256]{1,0:T(8,128)(2,1)S(1)}, bf16[384,256]{1,0:T(8,128)(2,1)S(1)}, u32[]{:S(2)}, u32[]{:S(2)}) %collective-permute-start.21) | collective-permute-done | bytes 196640 | tf_op jit(solution)/shard_map/back_2_cross/ppermute | solution.py:326
  106.6 0.8 collective-permute-start.22
  107.4 1.3 %collective-permute-done.22.refs_0_ = bf16[768,256]{1,0:T(8,128)(2,1)S(1)} collective-permute-done((bf16[768,256]{1,0:T(8,128)(2,1)S(1)}, bf16[768,256]{1,0:T(8,128)(2,1)S(1)}, u32[]{:S(2)}, u32[]{:S(2)}) %collective-permute-start.22) | collective-permute-done | bytes 393248 | tf_op jit(solution)/shard_map/swapped_2/ppermute | solution.py:326
  108.7 0.9 put.1
  (3 shorter events, 0.0 us)
Async XLA Ops:
  0.0 4.9 %copy-start = (bf16[128,3696]{0,1:T(8,128)(2,1)S(1)}, bf16[128,3696]{0,1:T(8,128)(2,1)}, u32[]{:S(2)}) copy-start(bf16[128,3696]{0,1:T(8,128)(2,1)} %param.4) | copy-start | bytes 2838532
  0.0 4.9 %copy-start.1 = (bf16[128,3696]{0,1:T(8,128)(2,1)S(1)}, bf16[128,3696]{0,1:T(8,128)(2,1)}, u32[]{:S(2)}) copy-start(bf16[128,3696]{0,1:T(8,128)(2,1)} %param.5) | copy-start | bytes 2838532
  2.3 8.8 %copy-start.2 = (bf16[256,256]{1,0:T(8,128)(2,1)S(1)}, bf16[256,256]{1,0:T(8,128)(2,1)}, u32[]{:S(2)}) copy-start(bf16[256,256]{1,0:T(8,128)(2,1)} %refs_0_) | copy-start | bytes 393220
  2.3 2.6 %collective-permute-start = (bf16[2944,128]{1,0:T(8,128)(2,1)}, bf16[2944,128]{1,0:T(8,128)(2,1)S(1)}, u32[]{:S(2)}, u32[]{:S(2)}) collective-permute-start(bf16[2944,128]{1,0:T(8,128)(2,1)} %cut.2), channel_id=1, source_target_pairs={{0,4},{4,0},{8,12},{12,8},{16,20},{20,16},{24,28},{28,24},{1,5},{5... | collective-permute-start | bytes 2261000 | tf_op jit(solution)/shard_map/swap/ppermute | solution.py:326
  5.4 21.3 %collective-permute-start.7 = (bf16[1408,256]{1,0:T(8,128)(2,1)S(1)}, bf16[1408,256]{1,0:T(8,128)(2,1)S(1)}, u32[]{:S(2)}, u32[]{:S(2)}) collective-permute-start(bf16[1408,256]{1,0:T(8,128)(2,1)S(1)} %get-tuple-element.31), channel_id=1, source_target_pairs={{0,8},{4,12},{24,16},{28,20},{1,9},{5,13},{25,17},{29,21},{2,10},{... | collective-permute-start | bytes 2162696 | tf_op jit(solution)/shard_map/outer_0/ppermute | solution.py:326
  10.3 29.6 %collective-permute-start.6 = (bf16[2944,256]{1,0:T(8,128)(2,1)S(1)}, bf16[2944,256]{1,0:T(8,128)(2,1)S(1)}, u32[]{:S(2)}, u32[]{:S(2)}) collective-permute-start(bf16[2944,256]{1,0:T(8,128)(2,1)S(1)} %get-tuple-element.35.refs_2_), channel_id=1, source_target_pairs={{8,16},{12,20},{16,8},{20,12},{9,17},{13,21},{17,9},{21,13},{10,18... | collective-permute-start | bytes 4521992 | tf_op jit(solution)/shard_map/own_01/ppermute | solution.py:326
  11.1 5.7 %collective-permute-start.1 = (bf16[256,256]{1,0:T(8,128)(2,1)S(1)}, bf16[256,256]{1,0:T(8,128)(2,1)S(1)}, u32[]{:S(2)}, u32[]{:S(2)}) collective-permute-start(bf16[256,256]{1,0:T(8,128)(2,1)S(1)} %copy-done.2), channel_id=1, source_target_pairs={{0,1},{1,0},{2,3},{3,2},{4,5},{5,4},{6,7},{7,6},{8,9},{9,8},{10,11... | collective-permute-start | bytes 393224 | tf_op jit(solution)/shard_map/ppermute | solution.py:350
  12.6 7.8 %collective-permute-start.2 = (bf16[256,256]{1,0:T(8,128)(2,1)S(1)}, bf16[256,256]{1,0:T(8,128)(2,1)S(1)}, u32[]{:S(2)}, u32[]{:S(2)}) collective-permute-start(bf16[256,256]{1,0:T(8,128)(2,1)S(1)} %copy-done.2), channel_id=1, source_target_pairs={{0,2},{1,3},{2,0},{3,1},{4,6},{5,7},{6,4},{7,5},{8,10},{9,11},{10,... | collective-permute-start | bytes 393224 | tf_op jit(solution)/shard_map/ppermute | solution.py:350
  14.2 6.3 %collective-permute-start.3 = (bf16[256,256]{1,0:T(8,128)(2,1)S(1)}, bf16[256,256]{1,0:T(8,128)(2,1)S(1)}, u32[]{:S(2)}, u32[]{:S(2)}) collective-permute-start(bf16[256,256]{1,0:T(8,128)(2,1)S(1)} %copy-done.2), channel_id=1, source_target_pairs={{0,3},{1,2},{2,1},{3,0},{4,7},{5,6},{6,5},{7,4},{8,11},{9,10},{10,... | collective-permute-start | bytes 393224 | tf_op jit(solution)/shard_map/ppermute | solution.py:350
  20.6 17.4 %collective-permute-start.4 = (bf16[1024,256]{1,0:T(8,128)(2,1)S(1)}, bf16[1024,256]{1,0:T(8,128)(2,1)S(1)}, u32[]{:S(2)}, u32[]{:S(2)}) collective-permute-start(bf16[1024,256]{1,0:T(8,128)(2,1)S(1)} %get-tuple-element.34), channel_id=1, source_target_pairs={{0,8},{4,12},{24,16},{28,20},{1,9},{5,13},{25,17},{29,21},{2,10},{... | collective-permute-start | bytes 1572872 | tf_op jit(solution)/shard_map/x_outer/ppermute | solution.py:326
  26.8 27.3 %collective-permute-start.10 = (bf16[1536,256]{1,0:T(8,128)(2,1)S(1)}, bf16[1536,256]{1,0:T(8,128)(2,1)S(1)}, u32[]{:S(2)}, u32[]{:S(2)}) collective-permute-start(bf16[1536,256]{1,0:T(8,128)(2,1)S(1)} %pack.4), channel_id=1, source_target_pairs={{0,8},{4,12},{24,16},{28,20},{1,9},{5,13},{25,17},{29,21},{2,10},{... | collective-permute-start | bytes 2359304 | tf_op jit(solution)/shard_map/outer_1/ppermute | solution.py:326
  38.0 1.9 %collective-permute-start.5 = (bf16[1024,256]{1,0:T(8,128)(2,1)S(1)}, bf16[1024,256]{1,0:T(8,128)(2,1)S(1)}, u32[]{:S(2)}, u32[]{:S(2)}) collective-permute-start(bf16[1024,256]{1,0:T(8,128)(2,1)S(1)} %collective-permute-done.4.refs_0_), channel_id=1, source_target_pairs={{0,4},{4,0},{8,12},{12,8},{16,20},{20,16},{24,28},{28,24},{1,5},{5... | collective-permute-start | bytes 1572872 | tf_op jit(solution)/shard_map/x_outer_other/ppermute | solution.py:326
  38.0 17.7 %collective-permute-start.8 = (bf16[1408,256]{1,0:T(8,128)(2,1)S(1)}, bf16[1408,256]{1,0:T(8,128)(2,1)S(1)}, u32[]{:S(2)}, u32[]{:S(2)}) collective-permute-start(bf16[1408,256]{1,0:T(8,128)(2,1)S(1)} %collective-permute-done.7.refs_4_), channel_id=1, source_target_pairs={{8,16},{12,20},{16,8},{20,12},{9,17},{13,21},{17,9},{21,13},{10,18... | collective-permute-start | bytes 2162696 | tf_op jit(solution)/shard_map/far_0/ppermute | solution.py:326
  54.0 14.7 %collective-permute-start.11 = (bf16[1536,256]{1,0:T(8,128)(2,1)S(1)}, bf16[1536,256]{1,0:T(8,128)(2,1)S(1)}, u32[]{:S(2)}, u32[]{:S(2)}) collective-permute-start(bf16[1536,256]{1,0:T(8,128)(2,1)S(1)} %collective-permute-done.10.refs_4_), channel_id=1, source_target_pairs={{8,16},{12,20},{16,8},{20,12},{9,17},{13,21},{17,9},{21,13},{10,18... | collective-permute-start | bytes 2359304 | tf_op jit(solution)/shard_map/far_1/ppermute | solution.py:326
  54.7 13.9 %collective-permute-start.9 = (bf16[1024,256]{1,0:T(8,128)(2,1)S(1)}, bf16[1024,256]{1,0:T(8,128)(2,1)S(1)}, u32[]{:S(2)}, u32[]{:S(2)}) collective-permute-start(bf16[1024,256]{1,0:T(8,128)(2,1)S(1)} %get-tuple-element.49.refs_0_), channel_id=1, source_target_pairs={{0,4},{4,0},{8,12},{12,8},{16,20},{20,16},{24,28},{28,24},{1,5},{5... | collective-permute-start | bytes 1572872 | tf_op jit(solution)/shard_map/x_other/ppermute | solution.py:326
  55.2 1.8 %collective-permute-start.12 = (bf16[768,128]{1,0:T(8,128)(2,1)S(1)}, bf16[768,128]{1,0:T(8,128)(2,1)S(1)}, u32[]{:S(2)}, u32[]{:S(2)}) collective-permute-start(bf16[768,128]{1,0:T(8,128)(2,1)S(1)} %cut.3), channel_id=1, source_target_pairs={{0,4},{4,0},{8,12},{12,8},{16,20},{20,16},{24,28},{28,24},{1,5},{5... | collective-permute-start | bytes 589832 | tf_op jit(solution)/shard_map/swap_rest/ppermute | solution.py:326
  55.7 24.9 %collective-permute-start.17 = (bf16[704,512]{1,0:T(8,128)(2,1)S(1)}, bf16[704,512]{1,0:T(8,128)(2,1)S(1)}, u32[]{:S(2)}, u32[]{:S(2)}) collective-permute-start(bf16[704,512]{1,0:T(8,128)(2,1)S(1)} %outer_hidden.3), channel_id=1, source_target_pairs={{8,0},{12,4},{16,24},{20,28},{9,1},{13,5},{17,25},{21,29},{10,2},{... | collective-permute-start | bytes 2162696 | tf_op jit(solution)/shard_map/back_0/ppermute | solution.py:326
  57.2 17.8 %collective-permute-start.14 = (bf16[768,256]{1,0:T(8,128)(2,1)S(1)}, bf16[768,256]{1,0:T(8,128)(2,1)S(1)}, u32[]{:S(2)}, u32[]{:S(2)}) collective-permute-start(bf16[768,256]{1,0:T(8,128)(2,1)S(1)} %pack.5.refs_2_), channel_id=1, source_target_pairs={{0,8},{4,12},{24,16},{28,20},{1,9},{5,13},{25,17},{29,21},{2,10},{... | collective-permute-start | bytes 1179656 | tf_op jit(solution)/shard_map/outer_2/ppermute | solution.py:326
  67.9 7.7 %collective-permute-start.13 = (bf16[768,256]{1,0:T(8,128)(2,1)S(1)}, bf16[768,256]{1,0:T(8,128)(2,1)S(1)}, u32[]{:S(2)}, u32[]{:S(2)}) collective-permute-start(bf16[768,256]{1,0:T(8,128)(2,1)S(1)} %pack.5.refs_2_), channel_id=1, source_target_pairs={{8,16},{12,20},{16,8},{20,12},{9,17},{13,21},{17,9},{21,13},{10,18... | collective-permute-start | bytes 1179656 | tf_op jit(solution)/shard_map/own_2/ppermute | solution.py:326
  68.8 30.2 %collective-permute-start.19 = (bf16[768,512]{1,0:T(8,128)(2,1)S(1)}, bf16[768,512]{1,0:T(8,128)(2,1)S(1)}, u32[]{:S(2)}, u32[]{:S(2)}) collective-permute-start(bf16[768,512]{1,0:T(8,128)(2,1)S(1)} %outer_hidden.4), channel_id=1, source_target_pairs={{8,0},{12,4},{16,24},{20,28},{9,1},{13,5},{17,25},{21,29},{10,2},{... | collective-permute-start | bytes 2359304 | tf_op jit(solution)/shard_map/back_1/ppermute | solution.py:326
  70.1 5.6 %collective-permute-start.16 = (bf16[704,256]{1,0:T(8,128)(2,1)S(1)}, bf16[704,256]{1,0:T(8,128)(2,1)S(1)}, u32[]{:S(2)}, u32[]{:S(2)}) collective-permute-start(bf16[704,256]{1,0:T(8,128)(2,1)S(1)} %get-tuple-element.37), channel_id=1, source_target_pairs={{0,4},{4,0},{8,12},{12,8},{16,20},{20,16},{24,28},{28,24},{1,5},{5... | collective-permute-start | bytes 1081352 | tf_op jit(solution)/shard_map/swapped_0/ppermute | solution.py:326
  75.0 6.5 %collective-permute-start.15 = (bf16[768,256]{1,0:T(8,128)(2,1)S(1)}, bf16[768,256]{1,0:T(8,128)(2,1)S(1)}, u32[]{:S(2)}, u32[]{:S(2)}) collective-permute-start(bf16[768,256]{1,0:T(8,128)(2,1)S(1)} %collective-permute-done.14.refs_4_), channel_id=1, source_target_pairs={{8,16},{12,20},{16,8},{20,12},{9,17},{13,21},{17,9},{21,13},{10,18... | collective-permute-start | bytes 1179656 | tf_op jit(solution)/shard_map/far_2/ppermute | solution.py:326
  81.4 2.7 %collective-permute-start.18 = (bf16[768,256]{1,0:T(8,128)(2,1)S(1)}, bf16[768,256]{1,0:T(8,128)(2,1)S(1)}, u32[]{:S(2)}, u32[]{:S(2)}) collective-permute-start(bf16[768,256]{1,0:T(8,128)(2,1)S(1)} %get-tuple-element.51), channel_id=1, source_target_pairs={{0,4},{4,0},{8,12},{12,8},{16,20},{20,16},{24,28},{28,24},{1,5},{5... | collective-permute-start | bytes 1179656 | tf_op jit(solution)/shard_map/swapped_1/ppermute | solution.py:326
  81.5 22.9 %collective-permute-start.20 = (bf16[384,256]{1,0:T(8,128)(2,1)S(1)}, bf16[384,256]{1,0:T(8,128)(2,1)S(1)}, u32[]{:S(2)}, u32[]{:S(2)}) collective-permute-start(bf16[384,256]{1,0:T(8,128)(2,1)S(1)} %get-tuple-element.47), channel_id=1, source_target_pairs={{8,0},{12,4},{16,24},{20,28},{9,1},{13,5},{17,25},{21,29},{10,2},{... | collective-permute-start | bytes 589832 | tf_op jit(solution)/shard_map/back_2_same/ppermute | solution.py:326
  82.8 23.8 %collective-permute-start.21 = (bf16[384,256]{1,0:T(8,128)(2,1)S(1)}, bf16[384,256]{1,0:T(8,128)(2,1)S(1)}, u32[]{:S(2)}, u32[]{:S(2)}) collective-permute-start(bf16[384,256]{1,0:T(8,128)(2,1)S(1)} %get-tuple-element.54), channel_id=1, source_target_pairs={{8,4},{12,0},{16,28},{20,24},{9,5},{13,1},{17,29},{21,25},{10,6},{... | collective-permute-start | bytes 589832 | tf_op jit(solution)/shard_map/back_2_cross/ppermute | solution.py:326
  106.6 2.2 %collective-permute-start.22 = (bf16[768,256]{1,0:T(8,128)(2,1)S(1)}, bf16[768,256]{1,0:T(8,128)(2,1)S(1)}, u32[]{:S(2)}, u32[]{:S(2)}) collective-permute-start(bf16[768,256]{1,0:T(8,128)(2,1)S(1)} %get-tuple-element.55), channel_id=1, source_target_pairs={{0,4},{4,0},{8,12},{12,8},{16,20},{20,16},{24,28},{28,24},{1,5},{5... | collective-permute-start | bytes 1179656 | tf_op jit(solution)/shard_map/swapped_2/ppermute | solution.py:326
